TPU v7x, 32 devices: a whole 2x2x4 slice. The times are simulated.
32 devices in a mesh: dom: 4 (over x, core), row: 8 (over z, y).
Axes of the slice: x: 2, y: 2, z: 4, core: 2. Of those that a mesh axis runs over, the one named last changes fastest.
Arguments:
- entity_table: float32 [4, 2048, 400], P('dom', 'row'), may hold values from -1.5 to 1.5
- adagrad_state: float32 [4, 2048], P('dom', 'row'), may hold values from 0.05 to 0.5
- relations: bfloat16 [16, 400], replicated, may hold values from -4 to 4
- sources: int32 [2, 4, 3072], P(None, 'dom', 'row'), may hold values from 0 to 2047, as said below
- targets: int32 [2, 4, 3072], P(None, 'dom', 'row'), may hold values from 0 to 2047, as said below
- relation_ids: int32 [2, 4, 3072], P(None, 'dom', 'row'), may hold values from 0 to 15
- edge_counts: int32 [2, 4, 8], P(None, 'dom', 'row'), may hold values from 96 to 384, as said below
Outputs:
- new_table: float32 [4, 2048, 400], P('dom', 'row')
- new_state: float32 [4, 2048], P('dom', 'row')
Inputs may be any that keep to these rules, and one draw needn't show every extreme that they name: `edge_counts`: in every round some aligned block is full, holding 384 live edges; the live edges of a block are its first slots. `sources`: in every round and bucket, the 384 slots of one aligned block name rows of any one run of 256 rows (rows with the same row div 256) at most 96 times, and in every block some run exactly 96 times. `targets`: in every round and bucket, the 384 slots of one aligned block name rows of any one run of 256 rows (rows with the same row div 256) at most 96 times, and in every block some run exactly 96 times.
All inputs are finite; a program needn't handle non-finite values.
Results may differ from a plain program's by a relative error of at most 0.0019.
Values may be sent and summed in bfloat16 or wider, within the bound.
No kernel may reach another device: no remote copies, remote signals or barrier semaphores. Data moves between devices by JAX's collectives and lax.ppermute only.
A program may use at most 64 MiB of HBM per device.

v0:
```python
import jax
import jax.numpy as jnp
from jax import lax
from jax.experimental import pallas as pl
from jax.experimental.pallas import tpu as pltpu
from jax.sharding import PartitionSpec as P

GROUP = 384
ROUNDS = 2
LANES = 128
CHUNK = 2 * LANES
NOBODY = 65535

learn_rate = 0.1

F32 = jnp.float32
BF16 = jnp.bfloat16
I32 = jnp.int32
VMEM = pl.BlockSpec(memory_space=pltpu.VMEM)
HBM = pl.BlockSpec(memory_space=pltpu.HBM)
PARAMS = pltpu.CompilerParams(vmem_limit_bytes=48 * 1024 * 1024)


def place(x, core, z, y):
    return (x * 2 + core) * 8 + z * 2 + y


PLACES = [(x, c, z, y) for x in range(2) for c in range(2) for z in range(4) for y in range(2)]


def route(target):
    return [(place(*at), place(*target(*at))) for at in PLACES]


def far_z(x, z, y):
    swap = (z & 1) ^ (z >> 1) ^ y
    return z ^ (3 * swap * (1 - x) + (1 + swap) * x)


FIRST = [
    route(lambda x, c, z, y: (x, c, z ^ 1, y) if c == 0 else (x, c, z, y ^ 1)),
    route(lambda x, c, z, y: (x, c, z ^ 2, y) if c == 0 else (x ^ 1, c, z, y)),
    route(lambda x, c, z, y: (x, c, z ^ 3, y) if c == 0 else (x ^ 1, c, z, y ^ 1)),
]
SWAP_CORE = route(lambda x, c, z, y: (x, c ^ 1, z, y))
SWAP_X = route(lambda x, c, z, y: (x ^ 1, c, z, y))
SWAP_Y = route(lambda x, c, z, y: (x, c, z, y ^ 1))
ALONG_Z = [route(lambda x, c, z, y, k=k: (x, c, z ^ k, y)) for k in (1, 2, 3)]
SECOND = [
    SWAP_Y,
    [(place(x ^ 1, c, far_z(x, z, y), y), place(x, c, z, y)) for x, c, z, y in PLACES],
    [(place(x ^ 1, c, far_z(x, z, y), y ^ 1), place(x, c, z, y)) for x, c, z, y in PLACES],
]


def move(value, pairs):
    return lax.ppermute(value, ("dom", "row"), pairs)


def back(pairs):
    return [(target, source) for source, target in pairs]


def here():
    dom = lax.axis_index("dom")
    row = lax.axis_index("row")
    return dom // 2, dom % 2, row // 2, row % 2


def halves(width):
    half = width // 2
    return half, -(-half // 16) * 16


def spread(value, padded):
    half = value.shape[0] // 2
    blank = jnp.zeros((padded - half, value.shape[1]), value.dtype)
    return jnp.concatenate([value[:half], blank, value[half:], blank], 0)


def open_kernel(
    entity_ref, count_ref, source_ref, target_ref, relation_ref, wire_ref, ids_ref, *scratch
):
    entity, counts, slots, sem = scratch
    refs = (source_ref, target_ref, relation_ref)
    copies = [pltpu.make_async_copy(refs[n], slots.at[n], sem.at[n]) for n in range(3)]
    copies.append(pltpu.make_async_copy(count_ref, counts, sem.at[3]))
    copies.append(pltpu.make_async_copy(entity_ref, entity, sem.at[4]))
    for copy in copies:
        copy.start()
    for copy in copies:
        copy.wait()
    wire_ref[...] = spread(entity[...], wire_ref.shape[0] // 2).astype(BF16)
    edge = lax.broadcasted_iota(I32, (1, ids_ref.shape[1]), 1)
    rows = []
    for round_index in range(ROUNDS):
        live = edge < counts[0:1, round_index : round_index + 1]
        rows.append(jnp.where(live, slots[0, round_index], -1))
        rows.append(jnp.where(live, slots[1, round_index], -1))
        rows.append(slots[2, round_index])
    ids_ref[...] = jnp.concatenate(rows + [jnp.zeros_like(edge)] * 2, 0)


def open_tables(entity, edge_counts, sources, targets, relation_ids):
    width, rows = entity.shape
    padded = halves(width)[1]
    slots = sources.shape[-1]
    return pl.pallas_call(
        open_kernel,
        out_shape=(
            jax.ShapeDtypeStruct((2 * padded, rows), BF16),
            jax.ShapeDtypeStruct((8, slots), I32),
        ),
        in_specs=[HBM] * 5,
        out_specs=(VMEM, VMEM),
        scratch_shapes=[
            pltpu.VMEM((width, rows), F32),
            pltpu.VMEM((1, ROUNDS), I32),
            pltpu.VMEM((3, ROUNDS, 1, slots), I32),
            pltpu.SemaphoreType.DMA((5,)),
        ],
        name="open_tables",
    )(entity, edge_counts.reshape(1, ROUNDS), sources, targets, relation_ids)


def lists_kernel(rows_per, own_ref, other_ref, relations_ref, out_ref, relate_ref):
    slots = own_ref.shape[-1]
    core = lax.axis_index("dom") % 2
    width = relations_ref.shape[1]
    half, padded = halves(width)
    full = -(-width // LANES) * LANES
    relations = jnp.pad(relations_ref[...].astype(F32), ((0, 0), (0, full - width)))
    relate_ref[...] = spread(relations.T[:width], padded).astype(BF16)
    lower = lax.broadcasted_iota(I32, (slots, slots), 0)
    upper = lax.broadcasted_iota(I32, (slots, slots), 1)
    before = (lower <= upper).astype(F32).astype(BF16)
    group_ids = lax.broadcasted_iota(I32, (4, slots), 0)
    edge = lax.broadcasted_iota(I32, (1, 2 * slots), 1)
    found = []
    for round_index in range(ROUNDS):
        for side in range(2):
            along_z = (core == side) if round_index == 0 else False
            parts = []
            for ref in (own_ref, other_ref):
                ids = ref[3 * round_index + side : 3 * round_index + side + 1, :]
                live = ids >= 0
                holder = jnp.where(live, ids // rows_per, 0)
                local = ids - holder * rows_per
                group = holder // 2
                which = holder % 2
                if round_index == 0:
                    group = jnp.where(along_z, holder // 4 * 2 + which, group)
                    which = jnp.where(along_z, holder // 2 % 2, which)
                mine = jnp.logical_and(group_ids == group, live)
                parts.append((live, local, group, which, mine))
            found.append(parts)
    masks = jnp.concatenate(
        [part[4].astype(F32) for parts in found for part in parts], 0
    ).astype(BF16)
    running = jnp.dot(masks, before, preferred_element_type=F32)
    main_ids = lax.broadcasted_iota(I32, (4 * CHUNK, 2 * slots), 0)
    rest_ids = lax.broadcasted_iota(I32, (4 * LANES, 2 * slots), 0) + 4 * CHUNK
    for n, parts in enumerate(found):
        round_index, side = n // 2, n % 2
        joined = []
        first_total = running[8 * n : 8 * n + 4, slots - 1 : slots]
        for which_block, (live, local, group, which, mine) in enumerate(parts):
            ranks = running[8 * n + 4 * which_block : 8 * n + 4 * which_block + 4]
            if which_block == 1:
                ranks = ranks + first_total
            rank = jnp.sum(jnp.where(mine, ranks, 0.0), axis=0, keepdims=True).astype(I32) - 1
            slot = jnp.where(
                rank < CHUNK, group * CHUNK + rank, 4 * CHUNK + group * LANES + rank - CHUNK
            )
            slot = jnp.where(live, slot, -1)
            joined.append((slot, local, which))
        slot, local, which = (
            jnp.concatenate([a, b], 1) for a, b in zip(joined[0], joined[1])
        )
        kind = jnp.concatenate(
            [ref[3 * round_index + 2 : 3 * round_index + 3, :] for ref in (own_ref, other_ref)], 1
        )
        values = jnp.concatenate(
            [local, which, kind, edge // 32, edge % 32, jnp.ones_like(edge)]
            + [jnp.zeros_like(edge)] * 2,
            0,
        ).astype(F32).astype(BF16)

        def place_rows(slot_ids, first_row):
            pick = (slot_ids == slot).astype(F32).astype(BF16)
            rows = lax.dot_general(
                values, pick, (((1,), (1,)), ((), ())), preferred_element_type=F32
            ).astype(I32)
            there = rows[5:6] > 0
            ids = jnp.where(there, rows[1:2] * rows_per + rows[0:1], NOBODY)
            packed = jnp.bitwise_or(ids, jnp.left_shift(rows[3:4] * 32 + rows[4:5], 16))
            for at in range(slot_ids.shape[0] // LANES):
                cut = slice(at * LANES, (at + 1) * LANES)
                row = first_row + at
                out_ref[round_index, 2 * side, row : row + 1, :] = packed[:, cut]
                if side == 0:
                    out_ref[round_index, 1, row : row + 1, :] = rows[2:3, cut]

        place_rows(main_ids, 0)
        out_ref[round_index, 2 * side, 8:12, :] = jnp.full((4, LANES), NOBODY, I32)
        if side == 0:
            out_ref[round_index, 1, 8:12, :] = jnp.zeros((4, LANES), I32)

        @pl.when(jnp.max(slot) >= 4 * CHUNK)
        def _():
            place_rows(rest_ids, 8)


def make_lists(own, other, relations, rows_per):
    width = relations.shape[1]

    def kernel(*refs):
        lists_kernel(rows_per, *refs)

    return pl.pallas_call(
        kernel,
        out_shape=(
            jax.ShapeDtypeStruct((ROUNDS, 3, 12, LANES), I32),
            jax.ShapeDtypeStruct((2 * halves(width)[1], relations.shape[0]), BF16),
        ),
        in_specs=[VMEM] * 3,
        out_specs=(VMEM, VMEM),
        compiler_params=PARAMS,
        name="make_lists",
    )(own, other, relations)


def both(left, right):
    return jnp.concatenate([left, right], 0)


def tile(source, target, relate, source_edge, target_edge):
    half = source.shape[0] // 2
    relate_re, relate_im = relate[:half], relate[half:]
    source_re, source_im = source[:half].astype(F32), source[half:].astype(F32)
    queries = both(
        source_re * relate_re - source_im * relate_im,
        source_re * relate_im + source_im * relate_re,
    ).astype(BF16)
    scores = lax.dot_general(
        queries, target, (((0,), (0,)), ((), ())), preferred_element_type=F32
    )
    edge_row = target_edge.astype(F32)
    edge_col = jnp.broadcast_to(source_edge.astype(F32), (8, source_edge.shape[1])).T[:, :1]
    bent = 0.5 * jnp.tanh(0.5 * scores)
    weights = jnp.where(
        edge_col == edge_row,
        bent - 0.5,
        jnp.where((edge_col < GROUP) == (edge_row < GROUP), (bent + 0.5) * (1.0 / GROUP), 0.0),
    ).astype(BF16)
    query_grad = lax.dot_general(
        target, weights, (((1,), (1,)), ((), ())), preferred_element_type=F32
    )
    target_grad = jnp.dot(queries, weights, preferred_element_type=F32).astype(BF16)
    grad_re, grad_im = query_grad[:half], query_grad[half:]
    source_grad = both(
        grad_re * relate_re + grad_im * relate_im,
        grad_im * relate_re - grad_re * relate_im,
    ).astype(BF16)
    return source_grad, target_grad


def wanted_lists(round_index):
    x, core, z, y = here()
    if round_index == 0:
        line = z // 2 * 2 + y
        other_line = (1 - z // 2) * 2 + y
        return [(0, core, line), (0, core, other_line), (0, 1 - core, z)]
    swap = (z % 2 + z // 2 + y) % 2
    far = jnp.bitwise_xor(z, jnp.where(x == 0, 3 * swap, 1 + swap))
    return [(0, 0, z), (0, 1, far), (1, 0, far), (1, 1, z)]


def tiles_kernel(round_index, *refs):
    count = 4 if round_index == 0 else 2
    list_refs, relations_ref, refs = refs[:count], refs[count], refs[count + 1 :]
    count = 8 if round_index == 0 else 4
    table_refs, out_refs = refs[:count], refs[count : 2 * count]
    lists, flags, tables, picks, values, sums = refs[2 * count :]
    padded, rows = table_refs[0].shape
    pairs = lists.shape[1]
    x, core, z, y = here()
    low = z % 2
    wanted = wanted_lists(round_index)
    total = len(wanted)
    for pair in range(pairs):
        if round_index == 0:
            lists[0, pair] = list_refs[pair][0]
        else:
            lists[0, pair] = list_refs[0][pair]
            lists[1, pair] = list_refs[1][pair]

    def choose(flag, first, second):
        return jnp.where(flag == 0, first, second)

    def lay(n, flag, first, second):
        tables[n, :, :rows] = choose(flag, first[...], second[...])
        tables[n, :, rows:] = choose(flag, second[...], first[...])

    if round_index == 0:
        near, far = table_refs[:4], table_refs[4:]

        @pl.when(core == 0)
        def _():
            lay(0, low, near[0], near[1])
            lay(1, low, near[2], near[3])
            lay(2, y, far[2], far[3])

        @pl.when(core == 1)
        def _():
            lay(0, low, far[0], far[1])
            lay(1, low, far[2], far[3])
            lay(2, y, near[0], near[1])
    else:
        for n, first in ((0, 0), (1, 2), (2, 2), (3, 0)):
            lay(n, y, table_refs[first], table_refs[first + 1])

    def packed_of(n, pair):
        bucket, side, group = wanted[n]
        return jnp.concatenate(
            [lists[bucket, pair, 2 * side, pl.ds(2 * group + j, 1), :] for j in range(2)], 1
        )

    def kinds_of(n, pair):
        bucket, _, group = wanted[n]
        return jnp.concatenate(
            [lists[bucket, pair, 1, pl.ds(2 * group + j, 1), :] for j in range(2)], 1
        )

    row_ids = lax.broadcasted_iota(I32, (2 * rows, CHUNK), 0)

    def pick_of(packed):
        return (row_ids == jnp.bitwise_and(packed, 65535)).astype(F32).astype(BF16)

    def relate_of(kinds):
        slots = lax.broadcasted_iota(I32, (relations_ref.shape[1], kinds.shape[1]), 0)
        chosen = (slots == kinds).astype(F32).astype(BF16)
        return jnp.dot(relations_ref[...], chosen, preferred_element_type=F32)

    for n in range(total):
        for pair in range(pairs):
            cut = slice(pair * CHUNK, (pair + 1) * CHUNK)
            picks[n, :, cut] = pick_of(packed_of(n, pair))
        values[n] = jnp.dot(tables[n], picks[n], preferred_element_type=F32).astype(BF16)

    def compute(pair, sources, targets):
        cut = slice(pair * CHUNK, (pair + 1) * CHUNK)

        def joined(chosen, get):
            return jnp.concatenate([get(n) for n in chosen], 1)

        def edges(chosen):
            return joined(chosen, lambda n: jnp.right_shift(packed_of(n, pair), 16))

        got = tile(
            joined(sources, lambda n: values[n, :, cut]),
            joined(targets, lambda n: values[n, :, cut]),
            relate_of(joined(sources, lambda n: kinds_of(n, pair))),
            edges(sources),
            edges(targets),
        )
        for chosen, grads in zip((sources, targets), got):
            for at, n in enumerate(chosen):
                values[n, :, cut] = grads[:, at * CHUNK : (at + 1) * CHUNK]

    if round_index == 0:

        @pl.when(core == 0)
        def _():
            for pair in range(pairs):
                compute(pair, (0, 1), (2,))

        @pl.when(core == 1)
        def _():
            for pair in range(pairs):
                compute(pair, (2,), (0, 1))
    else:
        for pair in range(pairs):
            compute(pair, (0,), (1,))
            compute(pair, (2,), (3,))

    def scatter(grads, pick):
        return lax.dot_general(grads, pick, (((1,), (1,)), ((), ())), preferred_element_type=F32)

    for n in range(total):
        sums[n] = scatter(values[n], picks[n])

    def late_row(n, pair, kind):
        bucket, _, group = wanted[n]
        return lists[bucket, pair, kind, pl.ds(8 + group, 1), :]

    def late_ids(n, pair):
        return jnp.bitwise_and(late_row(n, pair, 2 * wanted[n][1]), 65535)

    lowest = late_ids(0, 0)
    for n in range(total):
        for pair in range(pairs):
            lowest = jnp.minimum(lowest, late_ids(n, pair))

    @pl.when(jnp.min(lowest) < NOBODY)
    def _():
        for n in range(total):
            for pair in range(pairs):
                flags[n, pair] = (jnp.min(late_ids(n, pair)) < NOBODY).astype(I32)
        spare = jnp.full((1, LANES), NOBODY, I32)

        def one_of(options, at):
            value = options[0]
            for n in range(1, len(options)):
                value = jnp.where(at == n, options[n], value)
            return value

        def each(step, carry):
            pair, task, combo = step // 6, step // 3 % 2, step % 3
            if round_index == 0:
                chosen = (jnp.where(core == 0, task, 2), jnp.where(core == 0, 2, task))
            else:
                chosen = (2 * task, 2 * task + 1)
            late = (combo != 1, combo != 0)
            due = [
                jnp.logical_or(jnp.logical_not(late[side]), flags[chosen[side], pair] > 0)
                for side in range(2)
            ]

            @pl.when(jnp.logical_and(due[0], due[1]))
            def _():
                found = []
                for side in range(2):
                    main = one_of([packed_of(n, pair) for n in range(total)], chosen[side])
                    extra = one_of(
                        [late_row(n, pair, 2 * wanted[n][1]) for n in range(total)], chosen[side]
                    )
                    packed = jnp.where(late[side], jnp.concatenate([extra, spare], 1), main)
                    pick = pick_of(packed)
                    gathered = jnp.dot(tables[chosen[side]], pick, preferred_element_type=F32)
                    found.append((gathered.astype(BF16), pick, jnp.right_shift(packed, 16)))
                main = one_of([kinds_of(n, pair) for n in range(total)], chosen[0])
                extra = one_of([late_row(n, pair, 1) for n in range(total)], chosen[0])
                kinds = jnp.where(late[0], jnp.concatenate([extra, extra], 1), main)
                grads = tile(
                    found[0][0], found[1][0], relate_of(kinds), found[0][2], found[1][2]
                )
                for side in range(2):
                    sums[chosen[side]] += scatter(grads[side], found[side][1])

            return carry

        lax.fori_loop(0, pairs * 6, each, 0)

    def part(total, which):
        return choose(which, total[:, :rows], total[:, rows:])

    if round_index > 0:
        near = sums[0] + sums[3]
        far = sums[1] + sums[2]
        out_refs[0][...] = part(near, y)
        out_refs[1][...] = part(near, 1 - y).astype(BF16)
        out_refs[2][...] = part(far, y).astype(BF16)
        out_refs[3][...] = part(far, 1 - y).astype(BF16)
        return

    def put(outs, n, which):
        for k in range(2):
            outs[k][...] = part(sums[n], which if k == 0 else 1 - which).astype(outs[k].dtype)

    def clear(outs):
        for ref in outs:
            ref[...] = jnp.zeros(ref.shape, ref.dtype)

    @pl.when(core == 0)
    def _():
        put(out_refs[0:2], 0, low)
        put(out_refs[2:4], 1, low)
        clear(out_refs[4:6])
        put(out_refs[6:8], 2, y)

    @pl.when(core == 1)
    def _():
        put(out_refs[0:2], 2, y)
        clear(out_refs[2:4])
        put(out_refs[4:6], 0, low)
        put(out_refs[6:8], 1, low)


def tiles(round_index, lists, relations, tables):
    padded, rows = tables[0].shape
    total, pairs = 3 + round_index, 4

    def kernel(*refs):
        tiles_kernel(round_index, *refs)

    kinds = [F32] * 4 + [BF16] * 4 if round_index == 0 else [F32] + [BF16] * 3
    operands = (*lists, relations, *tables)
    return pl.pallas_call(
        kernel,
        out_shape=tuple(jax.ShapeDtypeStruct((padded, rows), kind) for kind in kinds),
        in_specs=[VMEM] * len(operands),
        out_specs=(VMEM,) * len(kinds),
        scratch_shapes=[
            pltpu.VMEM((2, pairs, 3, 12, LANES), I32),
            pltpu.SMEM((4, pairs), I32),
            pltpu.VMEM((total, padded, 2 * rows), BF16),
            pltpu.VMEM((total, 2 * rows, pairs * CHUNK), BF16),
            pltpu.VMEM((total, padded, pairs * CHUNK), BF16),
            pltpu.VMEM((total, padded, 2 * rows), F32),
        ],
        compiler_params=PARAMS,
        cost_estimate=pl.CostEstimate(
            flops=8_000_000_000, bytes_accessed=8_000_000, transcendentals=1_000_000
        ),
        name="tiles",
    )(*operands)


def update_kernel(master_ref, state_ref, own_ref, a_ref, b_ref, c_ref, *outs):
    width = master_ref.shape[0]
    half, padded = halves(width)
    gradient = (own_ref[...] + a_ref[...].astype(F32)) + (
        b_ref[...].astype(F32) + c_ref[...].astype(F32)
    )
    gradient = jnp.concatenate([gradient[:half], gradient[padded : padded + half]], 0)
    state = state_ref[...] + jnp.sum(gradient * gradient, axis=0, keepdims=True) / width
    master = master_ref[...] - gradient * (learn_rate / jnp.sqrt(state))
    outs[0][...] = master
    outs[1][...] = state
    if len(outs) > 2:
        outs[2][...] = spread(master, padded).astype(BF16)


def update(master, state, own, a, b, c, last):
    shapes = [(master.shape, F32), (state.shape, F32)]
    if not last:
        shapes.append((own.shape, BF16))
    return pl.pallas_call(
        update_kernel,
        out_shape=tuple(jax.ShapeDtypeStruct(*shape) for shape in shapes),
        in_specs=[VMEM] * 6,
        out_specs=(VMEM,) * len(shapes),
        compiler_params=PARAMS,
        name="update",
    )(master, state, own, a, b, c)


def tied(value, other):
    return lax.optimization_barrier((value, other))[0]


def tile_body(entity_table, adagrad_state, relations, sources, targets, relation_ids, edge_counts):
    rows = entity_table.shape[1]
    entity = entity_table[0].T
    state = adagrad_state
    wire, ids = open_tables(entity, edge_counts, sources, targets, relation_ids)

    other_ids = move(ids, SWAP_Y)
    near = [wire] + [move(wire, pairs) for pairs in FIRST]
    lists, relate = make_lists(ids, other_ids, relations, rows)
    lists = [lists] + [move(lists, pairs) for pairs in ALONG_Z]
    *near, _ = lax.optimization_barrier((*near, lists))
    far = [move(block, SWAP_CORE) for block in near]
    second_lists = jnp.stack([part[1] for part in lists])
    other_lists = move(second_lists, SWAP_X)

    first = lax.optimization_barrier((lists, second_lists))[0]
    outs = tiles(0, first, relate, near + far)
    outs, other_lists = lax.optimization_barrier((outs, other_lists))
    cross = [move(block, SWAP_CORE).astype(F32) for block in outs[4:]]
    parts = [
        move((outs[1 + k] + cross[1 + k]).astype(BF16), back(FIRST[k])) for k in range(3)
    ]
    entity, state, wire = update(entity, state, outs[0] + cross[0], *parts, False)

    near = [wire] + [move(wire, pairs) for pairs in SECOND]
    own, *parts = tiles(1, [second_lists, other_lists], relate, near)
    parts = [move(parts[k], back(SECOND[k])) for k in range(3)]
    entity, state = update(entity, state, own, *parts, True)
    return (entity.T[None], state)


def shifted(value, axis, steps):
    count = lax.axis_size(axis)
    pairs = [(source, (source + steps) % count) for source in range(count)]
    return lax.ppermute(value, axis, pairs)


def edge_grads(src_rows, dst_rows, rel_rows, live_mask):
    half_width = src_rows.shape[-1] // 2
    source = src_rows.astype(jnp.float32)
    relate = rel_rows.astype(jnp.float32)
    src_real = source[..., :half_width]
    src_imag = source[..., half_width:]
    rel_real = relate[..., :half_width]
    rel_imag = relate[..., half_width:]
    queries = jnp.concatenate(
        [src_real * rel_real - src_imag * rel_imag, src_real * rel_imag + src_imag * rel_real], -1
    ).astype(jnp.bfloat16)
    scores = jnp.einsum("bik,bjk->bij", queries, dst_rows, preferred_element_type=jnp.float32)
    block_size = scores.shape[-1]
    diagonal = jnp.arange(block_size)[:, None] == jnp.arange(block_size)[None, :]
    pair_mask = live_mask[:, :, None] * live_mask[:, None, :]
    weights = (
        jnp.where(diagonal, -jax.nn.sigmoid(-scores), jax.nn.sigmoid(scores) / block_size)
        * pair_mask
    ).astype(jnp.bfloat16)
    query_grad = jnp.einsum("bij,bjk->bik", weights, dst_rows, preferred_element_type=jnp.float32)
    dst_grad = jnp.einsum("bij,bik->bjk", weights, queries, preferred_element_type=jnp.float32)
    grad_real = query_grad[..., :half_width]
    grad_imag = query_grad[..., half_width:]
    src_grad = jnp.concatenate(
        [grad_real * rel_real + grad_imag * rel_imag, grad_imag * rel_real - grad_real * rel_imag],
        -1,
    )
    return (src_grad.astype(jnp.bfloat16), dst_grad.astype(jnp.bfloat16))


def slot_places(row_ids, rows_per, holders_total, capacity):
    holder = row_ids // rows_per
    onehot = (holder[:, None] == jnp.arange(holders_total)[None, :]).astype(jnp.int32)
    running = jnp.cumsum(onehot, axis=0)
    rank = jnp.sum(onehot * running, axis=-1) - 1
    place = holder * capacity + rank
    request = (
        jnp.zeros((holders_total * capacity,), jnp.int32).at[place].set(row_ids - holder * rows_per)
    )
    return (place, request.reshape(holders_total, capacity))


def plain_body(entity_table, adagrad_state, relations, sources, targets, relation_ids, edge_counts):
    entity = entity_table[0]
    adagrad = adagrad_state[0]
    rows_per = entity.shape[0]
    width = entity.shape[1]
    slot_total = sources.shape[-1]
    holders_total = lax.axis_size("row")
    capacity = 2 * slot_total // holders_total
    slot_ids = jnp.arange(slot_total)
    rel_columns = jnp.arange(relations.shape[0])
    for round_index in range(ROUNDS):
        shift_by = round_index + 1
        src_ids = sources[round_index, 0]
        dst_ids = targets[round_index, 0]
        live_total = edge_counts[round_index, 0, 0]
        live_mask = (slot_ids < live_total).astype(jnp.float32)
        rel_onehot = (relation_ids[round_index, 0][:, None] == rel_columns[None, :]).astype(
            jnp.bfloat16
        )
        rel_rows = jnp.dot(rel_onehot, relations, preferred_element_type=jnp.float32).astype(
            jnp.bfloat16
        )
        own_rows = entity.astype(jnp.bfloat16)
        src_place, src_request = slot_places(src_ids, rows_per, holders_total, capacity)
        dst_place, dst_request = slot_places(dst_ids, rows_per, holders_total, capacity)
        serve_table = shifted(own_rows, "dom", shift_by)
        wanted = (
            lax.all_to_all(src_request, "row", split_axis=0, concat_axis=0, tiled=True),
            lax.all_to_all(dst_request, "row", split_axis=0, concat_axis=0, tiled=True),
        )
        src_serve = jnp.take(own_rows, wanted[0].reshape(-1), axis=0).reshape(
            holders_total, capacity, width
        )
        dst_serve = jnp.take(serve_table, wanted[1].reshape(-1), axis=0).reshape(
            holders_total, capacity, width
        )
        answered = (
            lax.all_to_all(src_serve, "row", split_axis=0, concat_axis=0, tiled=True),
            lax.all_to_all(dst_serve, "row", split_axis=0, concat_axis=0, tiled=True),
        )
        dst_answer = answered[1]
        src_rows = jnp.take(answered[0].reshape(-1, width), src_place, axis=0)
        dst_rows = jnp.take(dst_answer.reshape(-1, width), dst_place, axis=0)
        src_grad, dst_grad = edge_grads(
            src_rows.reshape(-1, GROUP, width),
            dst_rows.reshape(-1, GROUP, width),
            rel_rows.reshape(-1, GROUP, width),
            live_mask.reshape(-1, GROUP),
        )
        src_grad = src_grad.reshape(slot_total, width)
        dst_grad = dst_grad.reshape(slot_total, width)
        blank = jnp.zeros((holders_total * capacity, width), jnp.bfloat16)
        src_buffer = blank.at[src_place].set(src_grad).reshape(holders_total, capacity, width)
        dst_buffer = blank.at[dst_place].set(dst_grad).reshape(holders_total, capacity, width)
        parts = (
            lax.all_to_all(src_buffer, "row", split_axis=0, concat_axis=0, tiled=True),
            lax.all_to_all(dst_buffer, "row", split_axis=0, concat_axis=0, tiled=True),
        )
        lhs_sum = jax.ops.segment_sum(
            parts[0].reshape(-1, width).astype(jnp.float32),
            wanted[0].reshape(-1),
            num_segments=rows_per,
        )
        other_sum = jax.ops.segment_sum(
            parts[1].reshape(-1, width).astype(jnp.float32),
            wanted[1].reshape(-1),
            num_segments=rows_per,
        )
        returned = shifted(other_sum, "dom", -shift_by)
        gradient = lhs_sum + returned
        adagrad = adagrad + jnp.mean(gradient * gradient, axis=-1)
        entity = entity - learn_rate * gradient / jnp.sqrt(adagrad)[:, None]
    return (entity[None], adagrad[None])


def solution(mesh):
    in_specs = (
        P("dom", "row", None),
        P("dom", "row"),
        P(),
        P(None, "dom", "row"),
        P(None, "dom", "row"),
        P(None, "dom", "row"),
        P(None, "dom", "row"),
    )
    out_specs = (P("dom", "row", None), P("dom", "row"))

    def body(entity_table, adagrad_state, relations, sources, *rest):
        fits = (
            (mesh.shape["dom"], mesh.shape["row"]) == (4, 8)
            and entity_table.shape[1] == 256
            and sources.shape[-1] == GROUP
        )
        chosen = tile_body if fits else plain_body
        return chosen(entity_table, adagrad_state, relations, sources, *rest)

    return jax.shard_map(body, mesh=mesh, in_specs=in_specs, out_specs=out_specs, check_vma=False)
```

profile of v0, /device:TPU:4, one launch (start us, length us, event | category | flops | bytes accessed | tf_op | source)
XLA Modules:
  0.0 85.3 jit_solution(8461381826891834575)
XLA Ops:
  0.6 1.8 %open_tables.1 = (bf16[416,256]{1,0:T(8,128)(2,1)}, s32[8,384]{1,0:T(8,128)}) custom-call(f32[400,256]{1,0:T(8,128)} %bitcast.7, s32[1,2]{1,0:T(1,128)} %bitcast.9, s32[2,1,384]{2,1,0:T(1,128)} %source_ref.1, s32[2,1,384]{2,1,0:T(1,128)} %target_ref.1, s32[2,1,384]{2,1,0:T(1,128)} %relation_ref.1), custom_call_target="tpu_custom_call" | custom-call | tf_op jit(solution)/shard_map/open_tables/pallas_call | solution.py:108
  2.5 1.6 %collective-permute-start.4 = (bf16[416,256]{1,0:T(8,128)(2,1)}, bf16[416,256]{1,0:T(8,128)(2,1)S(1)}, u32[]{:S(2)}, u32[]{:S(2)}) collective-permute-start(bf16[416,256]{1,0:T(8,128)(2,1)} %get-tuple-element.48.refs_5_), channel_id=1, source_target_pairs={{0,2},{1,3},{2,0},{3,1},{4,6},{5,7},{6,4},{7,5},{8,9},{9,8},{10,11... | collective-permute-start | bytes 638984 | tf_op jit(solution)/shard_map/ppermute | solution.py:57
  4.1 2.6 %collective-permute-start.5 = (bf16[416,256]{1,0:T(8,128)(2,1)}, bf16[416,256]{1,0:T(8,128)(2,1)S(1)}, u32[]{:S(2)}, u32[]{:S(2)}) collective-permute-start(bf16[416,256]{1,0:T(8,128)(2,1)} %get-tuple-element.48.refs_5_), channel_id=1, source_target_pairs={{0,4},{1,5},{2,6},{3,7},{4,0},{5,1},{6,2},{7,3},{8,24},{9,25},{10,... | collective-permute-start | bytes 638984 | tf_op jit(solution)/shard_map/ppermute | solution.py:57
  6.7 0.2 collective-permute-start.6
  6.9 0.3 collective-permute-start
  7.2 3.8 %collective-permute-done.refs_1_ = s32[8,384]{1,0:T(8,128)S(1)} collective-permute-done((s32[8,384]{1,0:T(8,128)}, s32[8,384]{1,0:T(8,128)S(1)}, u32[]{:S(2)}, u32[]{:S(2)}) %collective-permute-start) | collective-permute-done | bytes 12320 | tf_op jit(solution)/shard_map/ppermute | solution.py:57
  11.1 0.7 copy-done.6
  11.8 2.5 %make_lists.1 = (s32[2,3,12,128]{3,2,1,0:T(8,128)S(1)}, bf16[416,16]{1,0:T(8,128)(2,1)S(1)}) custom-call(s32[8,384]{1,0:T(8,128)S(1)} %copy-done.6, s32[8,384]{1,0:T(8,128)S(1)} %collective-permute-done.refs_1_, bf16[16,400]{1,0:T(8,128)(2,1)S(1)} %copy-done.1), custom_call_target="tpu_custom_call" | custom-call | tf_op jit(solution)/shard_map/make_lists/pallas_call | solution.py:220
  14.3 1.6 %collective-permute-start.1 = (s32[2,3,12,128]{3,2,1,0:T(8,128)S(1)}, s32[2,3,12,128]{3,2,1,0:T(8,128)S(1)}, u32[]{:S(2)}, u32[]{:S(2)}) collective-permute-start(s32[2,3,12,128]{3,2,1,0:T(8,128)S(1)} %get-tuple-element.42.refs_0_), channel_id=1, source_target_pairs={{0,2},{1,3},{2,0},{3,1},{4,6},{5,7},{6,4},{7,5},{8,10},{9,11},{10,... | collective-permute-start | bytes 110600 | tf_op jit(solution)/shard_map/ppermute | solution.py:57
  15.9 2.6 %collective-permute-start.2 = (s32[2,3,12,128]{3,2,1,0:T(8,128)S(1)}, s32[2,3,12,128]{3,2,1,0:T(8,128)S(1)}, u32[]{:S(2)}, u32[]{:S(2)}) collective-permute-start(s32[2,3,12,128]{3,2,1,0:T(8,128)S(1)} %get-tuple-element.42.refs_0_), channel_id=1, source_target_pairs={{0,4},{1,5},{2,6},{3,7},{4,0},{5,1},{6,2},{7,3},{8,12},{9,13},{10,... | collective-permute-start | bytes 110600 | tf_op jit(solution)/shard_map/ppermute | solution.py:57
  18.5 3.5 %collective-permute-start.3 = (s32[2,3,12,128]{3,2,1,0:T(8,128)S(1)}, s32[2,3,12,128]{3,2,1,0:T(8,128)S(1)}, u32[]{:S(2)}, u32[]{:S(2)}) collective-permute-start(s32[2,3,12,128]{3,2,1,0:T(8,128)S(1)} %get-tuple-element.42.refs_0_), channel_id=1, source_target_pairs={{0,6},{1,7},{2,4},{3,5},{4,2},{5,3},{6,0},{7,1},{8,14},{9,15},{10,... | collective-permute-start | bytes 110600 | tf_op jit(solution)/shard_map/ppermute | solution.py:57
  22.1 2.4 %collective-permute-done.3.refs_3_ = s32[2,3,12,128]{3,2,1,0:T(8,128)S(1)} collective-permute-done((s32[2,3,12,128]{3,2,1,0:T(8,128)S(1)}, s32[2,3,12,128]{3,2,1,0:T(8,128)S(1)}, u32[]{:S(2)}, u32[]{:S(2)}) %collective-permute-start.3) | collective-permute-done | bytes 36896 | tf_op jit(solution)/shard_map/ppermute | solution.py:57
  24.4 0.1 collective-permute-start.10
  24.5 0.5 collective-permute-start.7
  25.0 0.1 collective-permute-start.8
  25.1 0.4 collective-permute-start.9
  25.6 0.7 slice-done
  26.3 1.6 %collective-permute-start.11 = (s32[4,3,12,128]{3,2,1,0:T(8,128)S(1)}, s32[4,3,12,128]{3,2,1,0:T(8,128)S(1)}, u32[]{:S(2)}, u32[]{:S(2)}) collective-permute-start(s32[4,3,12,128]{3,2,1,0:T(8,128)S(1)} %pad_add_fusion.refs_0_), channel_id=1, source_target_pairs={{0,16},{1,17},{2,18},{3,19},{4,20},{5,21},{6,22},{7,23},{8,24},{9,... | collective-permute-start | bytes 221192 | tf_op jit(solution)/shard_map/ppermute | solution.py:57
  27.9 0.9 %copy-done.8 = bf16[416,256]{1,0:T(8,128)(2,1)S(1)} copy-done((bf16[416,256]{1,0:T(8,128)(2,1)S(1)}, bf16[416,256]{1,0:T(8,128)(2,1)}, u32[]{:S(2)}) %copy-start.8) | copy-done | bytes 213016
  28.8 7.6 %tiles.2 = (f32[416,256]{1,0:T(8,128)S(1)}, f32[416,256]{1,0:T(8,128)S(1)}, f32[416,256]{1,0:T(8,128)S(1)}, f32[416,256]{1,0:T(8,128)S(1)}, bf16[416,256]{1,0:T(...) custom-call(s32[2,3,12,128]{3,2,1,0:T(8,128)S(1)} %get-tuple-element.42.re, ...), custom_call_target="tpu_custom_call" | custom-call | flops 8000000000 | bytes 8000000 | tf_op jit(solution)/shard_map/tiles/pallas_call | solution.py:499
  36.5 0.1 collective-permute-start.17
  36.6 0.5 collective-permute-start.15
  37.0 0.1 collective-permute-start.13
  37.1 0.4 collective-permute-start.12
  37.6 0.4 collective-permute-done.17
  38.0 0.1 add_convert_fusion
  38.1 3.6 %collective-permute-start.18 = (bf16[416,256]{1,0:T(8,128)(2,1)S(1)}, bf16[416,256]{1,0:T(8,128)(2,1)S(1)}, u32[]{:S(2)}, u32[]{:S(2)}) collective-permute-start(bf16[416,256]{1,0:T(8,128)(2,1)S(1)} %add_convert_fusion), channel_id=1, source_target_pairs={{6,0},{7,1},{4,2},{5,3},{2,4},{3,5},{0,6},{1,7},{25,8},{24,9},{27,... | collective-permute-start | bytes 638984 | tf_op jit(solution)/shard_map/ppermute | solution.py:57
  41.7 0.1 add_convert_fusion.1
  41.7 0.1 collective-permute-start.16
  41.8 0.1 add_convert_fusion.2
  41.9 0.9 %collective-permute-start.14 = (bf16[416,256]{1,0:T(8,128)(2,1)S(1)}, bf16[416,256]{1,0:T(8,128)(2,1)S(1)}, u32[]{:S(2)}, u32[]{:S(2)}) collective-permute-start(bf16[416,256]{1,0:T(8,128)(2,1)S(1)} %add_convert_fusion.2), channel_id=1, source_target_pairs={{2,0},{3,1},{0,2},{1,3},{6,4},{7,5},{4,6},{5,7},{9,8},{8,9},{11,10... | collective-permute-start | bytes 638984 | tf_op jit(solution)/shard_map/ppermute | solution.py:57
  42.9 2.9 %collective-permute-done.18.c_ref = bf16[416,256]{1,0:T(8,128)(2,1)S(1)} collective-permute-done((bf16[416,256]{1,0:T(8,128)(2,1)S(1)}, bf16[416,256]{1,0:T(8,128)(2,1)S(1)}, u32[]{:S(2)}, u32[]{:S(2)}) %collective-permute-start.18) | collective-permute-done | bytes 213024 | tf_op jit(solution)/shard_map/ppermute | solution.py:57
  45.8 4.5 %collective-permute-done.16.b_ref = bf16[416,256]{1,0:T(8,128)(2,1)S(1)} collective-permute-done((bf16[416,256]{1,0:T(8,128)(2,1)S(1)}, bf16[416,256]{1,0:T(8,128)(2,1)S(1)}, u32[]{:S(2)}, u32[]{:S(2)}) %collective-permute-start.16) | collective-permute-done | bytes 213024 | tf_op jit(solution)/shard_map/ppermute | solution.py:57
  50.3 1.4 %collective-permute-done.14.a_ref = bf16[416,256]{1,0:T(8,128)(2,1)S(1)} collective-permute-done((bf16[416,256]{1,0:T(8,128)(2,1)S(1)}, bf16[416,256]{1,0:T(8,128)(2,1)S(1)}, u32[]{:S(2)}, u32[]{:S(2)}) %collective-permute-start.14) | collective-permute-done | bytes 213024 | tf_op jit(solution)/shard_map/ppermute | solution.py:57
  51.8 0.2 update.2
  52.0 0.1 collective-permute-start.19
  52.1 1.0 %collective-permute-start.20 = (bf16[416,256]{1,0:T(8,128)(2,1)S(1)}, bf16[416,256]{1,0:T(8,128)(2,1)S(1)}, u32[]{:S(2)}, u32[]{:S(2)}) collective-permute-start(bf16[416,256]{1,0:T(8,128)(2,1)S(1)} %get-tuple-element.71.refs_3_), channel_id=1, source_target_pairs={{16,0},{23,1},{20,2},{19,3},{18,4},{21,5},{22,6},{17,7},{24,8},{31... | collective-permute-start | bytes 638984 | tf_op jit(solution)/shard_map/ppermute | solution.py:57
  53.1 5.3 %collective-permute-start.21 = (bf16[416,256]{1,0:T(8,128)(2,1)S(1)}, bf16[416,256]{1,0:T(8,128)(2,1)S(1)}, u32[]{:S(2)}, u32[]{:S(2)}) collective-permute-start(bf16[416,256]{1,0:T(8,128)(2,1)S(1)} %get-tuple-element.71.refs_3_), channel_id=1, source_target_pairs={{17,0},{22,1},{21,2},{18,3},{19,4},{20,5},{23,6},{16,7},{25,8},{30... | collective-permute-start | bytes 638984 | tf_op jit(solution)/shard_map/ppermute | solution.py:57
  58.4 0.3 collective-permute-done.19.refs_4_
  58.7 2.1 %collective-permute-done.20.refs_5_ = bf16[416,256]{1,0:T(8,128)(2,1)S(1)} collective-permute-done((bf16[416,256]{1,0:T(8,128)(2,1)S(1)}, bf16[416,256]{1,0:T(8,128)(2,1)S(1)}, u32[]{:S(2)}, u32[]{:S(2)}) %collective-permute-start.20) | collective-permute-done | bytes 213024 | tf_op jit(solution)/shard_map/ppermute | solution.py:57
  60.8 1.8 %collective-permute-done.21.refs_6_ = bf16[416,256]{1,0:T(8,128)(2,1)S(1)} collective-permute-done((bf16[416,256]{1,0:T(8,128)(2,1)S(1)}, bf16[416,256]{1,0:T(8,128)(2,1)S(1)}, u32[]{:S(2)}, u32[]{:S(2)}) %collective-permute-start.21) | collective-permute-done | bytes 213024 | tf_op jit(solution)/shard_map/ppermute | solution.py:57
  62.6 9.4 %tiles.3 = (f32[416,256]{1,0:T(8,128)S(1)}, bf16[416,256]{1,0:T(8,128)(2,1)S(1)}, bf16[416,256]{1,0:T(8,128)(2,1)S(1)}, bf16[416,256]{1,0:T(8,128)(2,1)S(1)}) custom-call(s32[4,3,12,128]{3,2,1,0:T(8,128)S(1)} %pad_add_fusion.refs_0_, s32[4,3,12,128]{3,2,1,0:T(8,128)S(1)} %collective-permute-done.11.refs_1_, ...), custom_call_target="tpu_custom_call" | custom-call | flops 8000000000 | bytes 8000000 | tf_op jit(solution)/shard_map/tiles/pallas_call | solution.py:499
  72.0 1.0 %collective-permute-start.22 = (bf16[416,256]{1,0:T(8,128)(2,1)S(1)}, bf16[416,256]{1,0:T(8,128)(2,1)S(1)}, u32[]{:S(2)}, u32[]{:S(2)}) collective-permute-start(bf16[416,256]{1,0:T(8,128)(2,1)S(1)} %get-tuple-element.73), channel_id=1, source_target_pairs={{1,0},{0,1},{3,2},{2,3},{5,4},{4,5},{7,6},{6,7},{9,8},{8,9},{11,10... | collective-permute-start | bytes 638984 | tf_op jit(solution)/shard_map/ppermute | solution.py:57
  73.0 2.8 %collective-permute-start.23 = (bf16[416,256]{1,0:T(8,128)(2,1)S(1)}, bf16[416,256]{1,0:T(8,128)(2,1)S(1)}, u32[]{:S(2)}, u32[]{:S(2)}) collective-permute-start(bf16[416,256]{1,0:T(8,128)(2,1)S(1)} %get-tuple-element.74), channel_id=1, source_target_pairs={{0,16},{1,23},{2,20},{3,19},{4,18},{5,21},{6,22},{7,17},{8,24},{9,... | collective-permute-start | bytes 638984 | tf_op jit(solution)/shard_map/ppermute | solution.py:57
  75.8 1.4 %collective-permute-start.24 = (bf16[416,256]{1,0:T(8,128)(2,1)S(1)}, bf16[416,256]{1,0:T(8,128)(2,1)S(1)}, u32[]{:S(2)}, u32[]{:S(2)}) collective-permute-start(bf16[416,256]{1,0:T(8,128)(2,1)S(1)} %get-tuple-element.75), channel_id=1, source_target_pairs={{0,17},{1,22},{2,21},{3,18},{4,19},{5,20},{6,23},{7,16},{8,25},{9,... | collective-permute-start | bytes 638984 | tf_op jit(solution)/shard_map/ppermute | solution.py:57
  77.2 2.5 %collective-permute-done.22.a_ref = bf16[416,256]{1,0:T(8,128)(2,1)S(1)} collective-permute-done((bf16[416,256]{1,0:T(8,128)(2,1)S(1)}, bf16[416,256]{1,0:T(8,128)(2,1)S(1)}, u32[]{:S(2)}, u32[]{:S(2)}) %collective-permute-start.22) | collective-permute-done | bytes 213024 | tf_op jit(solution)/shard_map/ppermute | solution.py:57
  79.7 4.6 %collective-permute-done.24.c_ref = bf16[416,256]{1,0:T(8,128)(2,1)S(1)} collective-permute-done((bf16[416,256]{1,0:T(8,128)(2,1)S(1)}, bf16[416,256]{1,0:T(8,128)(2,1)S(1)}, u32[]{:S(2)}, u32[]{:S(2)}) %collective-permute-start.24) | collective-permute-done | bytes 213024 | tf_op jit(solution)/shard_map/ppermute | solution.py:57
  84.3 1.0 %update.3 = (f32[400,256]{1,0:T(8,128)}, f32[1,256]{1,0:T(1,128)}) custom-call(f32[400,256]{1,0:T(8,128)S(1)} %get-tuple-element.68.master_ref, f32[1,256]{1,0:T(1,128)S(1)} %get-tuple-element.69.state_ref, f32[416,256]{1,0:T(8,128)S(1)} %get-tuple-element.72.own_ref, bf16[416,256]{1,0:T(8,128)(2,1)S(1)} %collective-permute-done.22.a_ref, ...), custom_call_target="tpu_custom_call" | custom-call | tf_op jit(solution)/shard_map/update/pallas_call | solution.py:539
  (37 shorter events, 0.2 us)
Async XLA Ops:
  0.6 10.4 %copy-start.1 = (bf16[16,400]{1,0:T(8,128)(2,1)S(1)}, bf16[16,400]{1,0:T(8,128)(2,1)}, u32[]{:S(2)}) copy-start(bf16[16,400]{1,0:T(8,128)(2,1)} %refs_2_.1) | copy-start | bytes 38404
  2.5 21.9 %collective-permute-start.4 = (bf16[416,256]{1,0:T(8,128)(2,1)}, bf16[416,256]{1,0:T(8,128)(2,1)S(1)}, u32[]{:S(2)}, u32[]{:S(2)}) collective-permute-start(bf16[416,256]{1,0:T(8,128)(2,1)} %get-tuple-element.48.refs_5_), channel_id=1, source_target_pairs={{0,2},{1,3},{2,0},{3,1},{4,6},{5,7},{6,4},{7,5},{8,9},{9,8},{10,11... | collective-permute-start | bytes 638984 | tf_op jit(solution)/shard_map/ppermute | solution.py:57
  4.1 20.3 %collective-permute-start.5 = (bf16[416,256]{1,0:T(8,128)(2,1)}, bf16[416,256]{1,0:T(8,128)(2,1)S(1)}, u32[]{:S(2)}, u32[]{:S(2)}) collective-permute-start(bf16[416,256]{1,0:T(8,128)(2,1)} %get-tuple-element.48.refs_5_), channel_id=1, source_target_pairs={{0,4},{1,5},{2,6},{3,7},{4,0},{5,1},{6,2},{7,3},{8,24},{9,25},{10,... | collective-permute-start | bytes 638984 | tf_op jit(solution)/shard_map/ppermute | solution.py:57
  6.7 17.7 %collective-permute-start.6 = (bf16[416,256]{1,0:T(8,128)(2,1)}, bf16[416,256]{1,0:T(8,128)(2,1)S(1)}, u32[]{:S(2)}, u32[]{:S(2)}) collective-permute-start(bf16[416,256]{1,0:T(8,128)(2,1)} %get-tuple-element.48.refs_5_), channel_id=1, source_target_pairs={{0,6},{1,7},{2,4},{3,5},{4,2},{5,3},{6,0},{7,1},{8,25},{9,24},{10,... | collective-permute-start | bytes 638984 | tf_op jit(solution)/shard_map/ppermute | solution.py:57
  6.9 4.1 %collective-permute-start = (s32[8,384]{1,0:T(8,128)}, s32[8,384]{1,0:T(8,128)S(1)}, u32[]{:S(2)}, u32[]{:S(2)}) collective-permute-start(s32[8,384]{1,0:T(8,128)} %get-tuple-element.40.refs_0_), channel_id=1, source_target_pairs={{0,1},{1,0},{2,3},{3,2},{4,5},{5,4},{6,7},{7,6},{8,9},{9,8},{10,11... | collective-permute-start | bytes 36872 | tf_op jit(solution)/shard_map/ppermute | solution.py:57
  11.1 0.7 copy-start.6
  14.3 4.2 %collective-permute-start.1 = (s32[2,3,12,128]{3,2,1,0:T(8,128)S(1)}, s32[2,3,12,128]{3,2,1,0:T(8,128)S(1)}, u32[]{:S(2)}, u32[]{:S(2)}) collective-permute-start(s32[2,3,12,128]{3,2,1,0:T(8,128)S(1)} %get-tuple-element.42.refs_0_), channel_id=1, source_target_pairs={{0,2},{1,3},{2,0},{3,1},{4,6},{5,7},{6,4},{7,5},{8,10},{9,11},{10,... | collective-permute-start | bytes 110600 | tf_op jit(solution)/shard_map/ppermute | solution.py:57
  15.9 6.1 %collective-permute-start.2 = (s32[2,3,12,128]{3,2,1,0:T(8,128)S(1)}, s32[2,3,12,128]{3,2,1,0:T(8,128)S(1)}, u32[]{:S(2)}, u32[]{:S(2)}) collective-permute-start(s32[2,3,12,128]{3,2,1,0:T(8,128)S(1)} %get-tuple-element.42.refs_0_), channel_id=1, source_target_pairs={{0,4},{1,5},{2,6},{3,7},{4,0},{5,1},{6,2},{7,3},{8,12},{9,13},{10,... | collective-permute-start | bytes 110600 | tf_op jit(solution)/shard_map/ppermute | solution.py:57
  18.5 7.0 %copy-start.2 = (s32[2,3,12,128]{3,2,1,0:T(8,128)}, s32[2,3,12,128]{3,2,1,0:T(8,128)S(1)}, u32[]{:S(2)}) copy-start(s32[2,3,12,128]{3,2,1,0:T(8,128)S(1)} %collective-permute-done.1.refs_1_) | copy-start | bytes 110596
  18.5 5.9 %collective-permute-start.3 = (s32[2,3,12,128]{3,2,1,0:T(8,128)S(1)}, s32[2,3,12,128]{3,2,1,0:T(8,128)S(1)}, u32[]{:S(2)}, u32[]{:S(2)}) collective-permute-start(s32[2,3,12,128]{3,2,1,0:T(8,128)S(1)} %get-tuple-element.42.refs_0_), channel_id=1, source_target_pairs={{0,6},{1,7},{2,4},{3,5},{4,2},{5,3},{6,0},{7,1},{8,14},{9,15},{10,... | collective-permute-start | bytes 110600 | tf_op jit(solution)/shard_map/ppermute | solution.py:57
  22.1 3.5 %copy-start.4 = (s32[2,3,12,128]{3,2,1,0:T(8,128)}, s32[2,3,12,128]{3,2,1,0:T(8,128)S(1)}, u32[]{:S(2)}) copy-start(s32[2,3,12,128]{3,2,1,0:T(8,128)S(1)} %collective-permute-done.2.refs_2_) | copy-start | bytes 110596
  24.4 3.4 %collective-permute-start.10 = (bf16[416,256]{1,0:T(8,128)(2,1)S(1)}, bf16[416,256]{1,0:T(8,128)(2,1)S(1)}, u32[]{:S(2)}, u32[]{:S(2)}) collective-permute-start(bf16[416,256]{1,0:T(8,128)(2,1)S(1)} %collective-permute-done.6.refs_8_), channel_id=1, source_target_pairs={{0,8},{1,9},{2,10},{3,11},{4,12},{5,13},{6,14},{7,15},{8,0},{9,1},... | collective-permute-start | bytes 638984 | tf_op jit(solution)/shard_map/ppermute | solution.py:57
  24.5 3.4 %collective-permute-start.7 = (bf16[416,256]{1,0:T(8,128)(2,1)}, bf16[416,256]{1,0:T(8,128)(2,1)S(1)}, u32[]{:S(2)}, u32[]{:S(2)}) collective-permute-start(bf16[416,256]{1,0:T(8,128)(2,1)} %get-tuple-element.48.refs_5_), channel_id=1, source_target_pairs={{0,8},{1,9},{2,10},{3,11},{4,12},{5,13},{6,14},{7,15},{8,0},{9,1},... | collective-permute-start | bytes 638984 | tf_op jit(solution)/shard_map/ppermute | solution.py:57
  25.0 2.9 %collective-permute-start.8 = (bf16[416,256]{1,0:T(8,128)(2,1)S(1)}, bf16[416,256]{1,0:T(8,128)(2,1)S(1)}, u32[]{:S(2)}, u32[]{:S(2)}) collective-permute-start(bf16[416,256]{1,0:T(8,128)(2,1)S(1)} %collective-permute-done.4.refs_6_), channel_id=1, source_target_pairs={{0,8},{1,9},{2,10},{3,11},{4,12},{5,13},{6,14},{7,15},{8,0},{9,1},... | collective-permute-start | bytes 638984 | tf_op jit(solution)/shard_map/ppermute | solution.py:57
  25.1 2.8 %collective-permute-start.9 = (bf16[416,256]{1,0:T(8,128)(2,1)S(1)}, bf16[416,256]{1,0:T(8,128)(2,1)S(1)}, u32[]{:S(2)}, u32[]{:S(2)}) collective-permute-start(bf16[416,256]{1,0:T(8,128)(2,1)S(1)} %collective-permute-done.5.refs_7_), channel_id=1, source_target_pairs={{0,8},{1,9},{2,10},{3,11},{4,12},{5,13},{6,14},{7,15},{8,0},{9,1},... | collective-permute-start | bytes 638984 | tf_op jit(solution)/shard_map/ppermute | solution.py:57
  25.5 0.7 slice-start
  25.5 0.7 slice-start.1
  26.3 1.6 %copy-start.3 = (s32[2,3,12,128]{3,2,1,0:T(8,128)S(1)}, s32[2,3,12,128]{3,2,1,0:T(8,128)}, u32[]{:S(2)}) copy-start(s32[2,3,12,128]{3,2,1,0:T(8,128)} %copy-done.2) | copy-start | bytes 110596
  26.3 1.6 %copy-start.5 = (s32[2,3,12,128]{3,2,1,0:T(8,128)S(1)}, s32[2,3,12,128]{3,2,1,0:T(8,128)}, u32[]{:S(2)}) copy-start(s32[2,3,12,128]{3,2,1,0:T(8,128)} %copy-done.4) | copy-start | bytes 110596
  26.3 10.2 %collective-permute-start.11 = (s32[4,3,12,128]{3,2,1,0:T(8,128)S(1)}, s32[4,3,12,128]{3,2,1,0:T(8,128)S(1)}, u32[]{:S(2)}, u32[]{:S(2)}) collective-permute-start(s32[4,3,12,128]{3,2,1,0:T(8,128)S(1)} %pad_add_fusion.refs_0_), channel_id=1, source_target_pairs={{0,16},{1,17},{2,18},{3,19},{4,20},{5,21},{6,22},{7,23},{8,24},{9,... | collective-permute-start | bytes 221192 | tf_op jit(solution)/shard_map/ppermute | solution.py:57
  27.9 0.9 %copy-start.8 = (bf16[416,256]{1,0:T(8,128)(2,1)S(1)}, bf16[416,256]{1,0:T(8,128)(2,1)}, u32[]{:S(2)}) copy-start(bf16[416,256]{1,0:T(8,128)(2,1)} %get-tuple-element.48.refs_5_) | copy-start | bytes 638980
  36.5 1.5 %collective-permute-start.17 = (bf16[416,256]{1,0:T(8,128)(2,1)S(1)}, bf16[416,256]{1,0:T(8,128)(2,1)S(1)}, u32[]{:S(2)}, u32[]{:S(2)}) collective-permute-start(bf16[416,256]{1,0:T(8,128)(2,1)S(1)} %get-tuple-element.67), channel_id=1, source_target_pairs={{0,8},{1,9},{2,10},{3,11},{4,12},{5,13},{6,14},{7,15},{8,0},{9,1},... | collective-permute-start | bytes 638984 | tf_op jit(solution)/shard_map/ppermute | solution.py:57
  36.6 5.1 %collective-permute-start.15 = (bf16[416,256]{1,0:T(8,128)(2,1)S(1)}, bf16[416,256]{1,0:T(8,128)(2,1)S(1)}, u32[]{:S(2)}, u32[]{:S(2)}) collective-permute-start(bf16[416,256]{1,0:T(8,128)(2,1)S(1)} %get-tuple-element.65), channel_id=1, source_target_pairs={{0,8},{1,9},{2,10},{3,11},{4,12},{5,13},{6,14},{7,15},{8,0},{9,1},... | collective-permute-start | bytes 638984 | tf_op jit(solution)/shard_map/ppermute | solution.py:57
  37.0 4.8 %collective-permute-start.13 = (bf16[416,256]{1,0:T(8,128)(2,1)S(1)}, bf16[416,256]{1,0:T(8,128)(2,1)S(1)}, u32[]{:S(2)}, u32[]{:S(2)}) collective-permute-start(bf16[416,256]{1,0:T(8,128)(2,1)S(1)} %get-tuple-element.63), channel_id=1, source_target_pairs={{0,8},{1,9},{2,10},{3,11},{4,12},{5,13},{6,14},{7,15},{8,0},{9,1},... | collective-permute-start | bytes 638984 | tf_op jit(solution)/shard_map/ppermute | solution.py:57
  37.1 5.7 %collective-permute-start.12 = (bf16[416,256]{1,0:T(8,128)(2,1)S(1)}, bf16[416,256]{1,0:T(8,128)(2,1)S(1)}, u32[]{:S(2)}, u32[]{:S(2)}) collective-permute-start(bf16[416,256]{1,0:T(8,128)(2,1)S(1)} %get-tuple-element.61), channel_id=1, source_target_pairs={{0,8},{1,9},{2,10},{3,11},{4,12},{5,13},{6,14},{7,15},{8,0},{9,1},... | collective-permute-start | bytes 638984 | tf_op jit(solution)/shard_map/ppermute | solution.py:57
  38.1 7.7 %collective-permute-start.18 = (bf16[416,256]{1,0:T(8,128)(2,1)S(1)}, bf16[416,256]{1,0:T(8,128)(2,1)S(1)}, u32[]{:S(2)}, u32[]{:S(2)}) collective-permute-start(bf16[416,256]{1,0:T(8,128)(2,1)S(1)} %add_convert_fusion), channel_id=1, source_target_pairs={{6,0},{7,1},{4,2},{5,3},{2,4},{3,5},{0,6},{1,7},{25,8},{24,9},{27,... | collective-permute-start | bytes 638984 | tf_op jit(solution)/shard_map/ppermute | solution.py:57
  41.7 8.6 %collective-permute-start.16 = (bf16[416,256]{1,0:T(8,128)(2,1)S(1)}, bf16[416,256]{1,0:T(8,128)(2,1)S(1)}, u32[]{:S(2)}, u32[]{:S(2)}) collective-permute-start(bf16[416,256]{1,0:T(8,128)(2,1)S(1)} %add_convert_fusion.1), channel_id=1, source_target_pairs={{4,0},{5,1},{6,2},{7,3},{0,4},{1,5},{2,6},{3,7},{24,8},{25,9},{26,... | collective-permute-start | bytes 638984 | tf_op jit(solution)/shard_map/ppermute | solution.py:57
  41.9 9.9 %copy-start = (f32[1,256,400]{1,2,0:T(8,128)S(1)}, f32[1,256,400]{1,2,0:T(8,128)}, u32[]{:S(2)}) copy-start(f32[1,256,400]{1,2,0:T(8,128)} %param.7) | copy-start | bytes 1228804
  41.9 9.9 %copy-start.7 = (f32[1,256]{1,0:T(1,128)S(1)}, f32[1,256]{1,0:T(1,128)}, u32[]{:S(2)}) copy-start(f32[1,256]{1,0:T(1,128)} %state_ref.1) | copy-start | bytes 3076
  41.9 9.9 %collective-permute-start.14 = (bf16[416,256]{1,0:T(8,128)(2,1)S(1)}, bf16[416,256]{1,0:T(8,128)(2,1)S(1)}, u32[]{:S(2)}, u32[]{:S(2)}) collective-permute-start(bf16[416,256]{1,0:T(8,128)(2,1)S(1)} %add_convert_fusion.2), channel_id=1, source_target_pairs={{2,0},{3,1},{0,2},{1,3},{6,4},{7,5},{4,6},{5,7},{9,8},{8,9},{11,10... | collective-permute-start | bytes 638984 | tf_op jit(solution)/shard_map/ppermute | solution.py:57
  52.0 6.7 %collective-permute-start.19 = (bf16[416,256]{1,0:T(8,128)(2,1)S(1)}, bf16[416,256]{1,0:T(8,128)(2,1)S(1)}, u32[]{:S(2)}, u32[]{:S(2)}) collective-permute-start(bf16[416,256]{1,0:T(8,128)(2,1)S(1)} %get-tuple-element.71.refs_3_), channel_id=1, source_target_pairs={{0,1},{1,0},{2,3},{3,2},{4,5},{5,4},{6,7},{7,6},{8,9},{9,8},{10,11... | collective-permute-start | bytes 638984 | tf_op jit(solution)/shard_map/ppermute | solution.py:57
  52.1 8.7 %collective-permute-start.20 = (bf16[416,256]{1,0:T(8,128)(2,1)S(1)}, bf16[416,256]{1,0:T(8,128)(2,1)S(1)}, u32[]{:S(2)}, u32[]{:S(2)}) collective-permute-start(bf16[416,256]{1,0:T(8,128)(2,1)S(1)} %get-tuple-element.71.refs_3_), channel_id=1, source_target_pairs={{16,0},{23,1},{20,2},{19,3},{18,4},{21,5},{22,6},{17,7},{24,8},{31... | collective-permute-start | bytes 638984 | tf_op jit(solution)/shard_map/ppermute | solution.py:57
  53.1 9.5 %collective-permute-start.21 = (bf16[416,256]{1,0:T(8,128)(2,1)S(1)}, bf16[416,256]{1,0:T(8,128)(2,1)S(1)}, u32[]{:S(2)}, u32[]{:S(2)}) collective-permute-start(bf16[416,256]{1,0:T(8,128)(2,1)S(1)} %get-tuple-element.71.refs_3_), channel_id=1, source_target_pairs={{17,0},{22,1},{21,2},{18,3},{19,4},{20,5},{23,6},{16,7},{25,8},{30... | collective-permute-start | bytes 638984 | tf_op jit(solution)/shard_map/ppermute | solution.py:57
  72.0 7.6 %collective-permute-start.22 = (bf16[416,256]{1,0:T(8,128)(2,1)S(1)}, bf16[416,256]{1,0:T(8,128)(2,1)S(1)}, u32[]{:S(2)}, u32[]{:S(2)}) collective-permute-start(bf16[416,256]{1,0:T(8,128)(2,1)S(1)} %get-tuple-element.73), channel_id=1, source_target_pairs={{1,0},{0,1},{3,2},{2,3},{5,4},{4,5},{7,6},{6,7},{9,8},{8,9},{11,10... | collective-permute-start | bytes 638984 | tf_op jit(solution)/shard_map/ppermute | solution.py:57
  73.0 6.7 %collective-permute-start.23 = (bf16[416,256]{1,0:T(8,128)(2,1)S(1)}, bf16[416,256]{1,0:T(8,128)(2,1)S(1)}, u32[]{:S(2)}, u32[]{:S(2)}) collective-permute-start(bf16[416,256]{1,0:T(8,128)(2,1)S(1)} %get-tuple-element.74), channel_id=1, source_target_pairs={{0,16},{1,23},{2,20},{3,19},{4,18},{5,21},{6,22},{7,17},{8,24},{9,... | collective-permute-start | bytes 638984 | tf_op jit(solution)/shard_map/ppermute | solution.py:57
  75.8 8.5 %collective-permute-start.24 = (bf16[416,256]{1,0:T(8,128)(2,1)S(1)}, bf16[416,256]{1,0:T(8,128)(2,1)S(1)}, u32[]{:S(2)}, u32[]{:S(2)}) collective-permute-start(bf16[416,256]{1,0:T(8,128)(2,1)S(1)} %get-tuple-element.75), channel_id=1, source_target_pairs={{0,17},{1,22},{2,21},{3,18},{4,19},{5,20},{6,23},{7,16},{8,25},{9,... | collective-permute-start | bytes 638984 | tf_op jit(solution)/shard_map/ppermute | solution.py:57
where the time goes:
time: 85.8 us; the launch traced here: 85.3 us
  starting transfers between devices  32.3 us (38%)
  waiting for transfers between devices  26.9 us (31%)
  Pallas kernels  22.6 us (26%)
  local copies, waits for them, and re-layouts  2.4 us (3%)
    ppermute x25, starting transfers between devices, move(): return lax.ppermute(value, ('dom', 'row'), pairs)  32.3 us
    ppermute x25, waiting for transfers between devices, move(): return lax.ppermute(value, ('dom', 'row'), pairs)  26.9 us
    pallas_call x2, Pallas kernels, tiles(): pl.pallas_call(kernel, out_shape=tuple((jax.ShapeDtypeStruct((padded, row...  17.1 us
    pallas_call x1, Pallas kernels, make_lists(): pl.pallas_call(kernel, out_shape=(jax.ShapeDtypeStruct((ROUNDS, 3, 12, LA...  2.52 us
    pallas_call x1, Pallas kernels, open_tables(): pl.pallas_call(open_kernel, out_shape=(jax.ShapeDtypeStruct((2 * padded,...  1.82 us
  transfers between devices with their start and end apart: 25, of which 12 were waited for; matrix products, arithmetic and copies ran while one was open for 0% of the time, Pallas kernels for 12%

commit v1 on v0

--- a/solution.py
+++ b/solution.py
@@ -10,6 +10,7 @@
 LANES = 128
 CHUNK = 2 * LANES
 NOBODY = 65535
+DEAD = 32767
 
 learn_rate = 0.1
 
@@ -45,7 +46,6 @@
 SWAP_CORE = route(lambda x, c, z, y: (x, c ^ 1, z, y))
 SWAP_X = route(lambda x, c, z, y: (x ^ 1, c, z, y))
 SWAP_Y = route(lambda x, c, z, y: (x, c, z, y ^ 1))
-ALONG_Z = [route(lambda x, c, z, y, k=k: (x, c, z ^ k, y)) for k in (1, 2, 3)]
 SECOND = [
     SWAP_Y,
     [(place(x ^ 1, c, far_z(x, z, y), y), place(x, c, z, y)) for x, c, z, y in PLACES],
@@ -91,17 +91,21 @@
     for copy in copies:
         copy.wait()
     wire_ref[...] = spread(entity[...], wire_ref.shape[0] // 2).astype(BF16)
-    edge = lax.broadcasted_iota(I32, (1, ids_ref.shape[1]), 1)
-    rows = []
+    edge = lax.broadcasted_iota(I32, (1, ids_ref.shape[2]), 1)
+    rows, kinds = [], []
     for round_index in range(ROUNDS):
         live = edge < counts[0:1, round_index : round_index + 1]
-        rows.append(jnp.where(live, slots[0, round_index], -1))
-        rows.append(jnp.where(live, slots[1, round_index], -1))
-        rows.append(slots[2, round_index])
-    ids_ref[...] = jnp.concatenate(rows + [jnp.zeros_like(edge)] * 2, 0)
-
-
-def open_tables(entity, edge_counts, sources, targets, relation_ids):
+        source = jnp.where(live, slots[0, round_index], DEAD)
+        target = jnp.where(live, slots[1, round_index], DEAD)
+        rows.append(jnp.bitwise_or(source, jnp.left_shift(target, 16)))
+        kinds.append(slots[2, round_index])
+    rows.append(jnp.bitwise_or(kinds[0], jnp.left_shift(kinds[1], 16)))
+    ids = jnp.concatenate(rows + [jnp.zeros_like(edge)], 0)
+    for n in range(ids_ref.shape[0]):
+        ids_ref[n] = ids
+
+
+def open_tables(entity, edge_counts, sources, targets, relation_ids, copies):
     width, rows = entity.shape
     padded = halves(width)[1]
     slots = sources.shape[-1]
@@ -109,7 +113,7 @@
         open_kernel,
         out_shape=(
             jax.ShapeDtypeStruct((2 * padded, rows), BF16),
-            jax.ShapeDtypeStruct((8, slots), I32),
+            jax.ShapeDtypeStruct((copies, 4, slots), I32),
         ),
         in_specs=[HBM] * 5,
         out_specs=(VMEM, VMEM),
@@ -123,111 +127,162 @@
     )(entity, edge_counts.reshape(1, ROUNDS), sources, targets, relation_ids)
 
 
-def lists_kernel(rows_per, own_ref, other_ref, relations_ref, out_ref, relate_ref):
-    slots = own_ref.shape[-1]
-    core = lax.axis_index("dom") % 2
-    width = relations_ref.shape[1]
-    half, padded = halves(width)
-    full = -(-width // LANES) * LANES
-    relations = jnp.pad(relations_ref[...].astype(F32), ((0, 0), (0, full - width)))
-    relate_ref[...] = spread(relations.T[:width], padded).astype(BF16)
+def wanted_lists(round_index):
+    x, core, z, y = here()
+    if round_index == 0:
+        line = z // 2 * 2 + y
+        other_line = (1 - z // 2) * 2 + y
+        return [(0, core, line), (0, core, other_line), (0, 1 - core, z)]
+    swap = (z % 2 + z // 2 + y) % 2
+    far = jnp.bitwise_xor(z, jnp.where(x == 0, 3 * swap, 1 + swap))
+    return [(0, 0, z), (0, 1, far), (1, 0, far), (1, 1, z)]
+
+
+def lists_kernel(round_index, rows_per, *refs):
+    buckets = 1 if round_index == 0 else 2
+    id_refs, (relations_ref, out_ref, *relate_ref) = refs[:buckets], refs[buckets:]
+    blocks, _, slots = id_refs[0].shape
+    pairs = blocks // 2
+    lists = wanted_lists(round_index)
+    if relate_ref:
+        width = relations_ref.shape[1]
+        half, padded = halves(width)
+        full = -(-width // LANES) * LANES
+        relations = jnp.pad(relations_ref[...].astype(F32), ((0, 0), (0, full - width)))
+        relate_ref[0][...] = spread(relations.T[:width], padded).astype(BF16)
     lower = lax.broadcasted_iota(I32, (slots, slots), 0)
     upper = lax.broadcasted_iota(I32, (slots, slots), 1)
     before = (lower <= upper).astype(F32).astype(BF16)
-    group_ids = lax.broadcasted_iota(I32, (4, slots), 0)
-    edge = lax.broadcasted_iota(I32, (1, 2 * slots), 1)
-    found = []
-    for round_index in range(ROUNDS):
-        for side in range(2):
-            along_z = (core == side) if round_index == 0 else False
-            parts = []
-            for ref in (own_ref, other_ref):
-                ids = ref[3 * round_index + side : 3 * round_index + side + 1, :]
-                live = ids >= 0
-                holder = jnp.where(live, ids // rows_per, 0)
-                local = ids - holder * rows_per
-                group = holder // 2
-                which = holder % 2
-                if round_index == 0:
-                    group = jnp.where(along_z, holder // 4 * 2 + which, group)
-                    which = jnp.where(along_z, holder // 2 % 2, which)
-                mine = jnp.logical_and(group_ids == group, live)
-                parts.append((live, local, group, which, mine))
-            found.append(parts)
-    masks = jnp.concatenate(
-        [part[4].astype(F32) for parts in found for part in parts], 0
-    ).astype(BF16)
-    running = jnp.dot(masks, before, preferred_element_type=F32)
-    main_ids = lax.broadcasted_iota(I32, (4 * CHUNK, 2 * slots), 0)
-    rest_ids = lax.broadcasted_iota(I32, (4 * LANES, 2 * slots), 0) + 4 * CHUNK
-    for n, parts in enumerate(found):
-        round_index, side = n // 2, n % 2
-        joined = []
-        first_total = running[8 * n : 8 * n + 4, slots - 1 : slots]
-        for which_block, (live, local, group, which, mine) in enumerate(parts):
-            ranks = running[8 * n + 4 * which_block : 8 * n + 4 * which_block + 4]
-            if which_block == 1:
-                ranks = ranks + first_total
-            rank = jnp.sum(jnp.where(mine, ranks, 0.0), axis=0, keepdims=True).astype(I32) - 1
-            slot = jnp.where(
-                rank < CHUNK, group * CHUNK + rank, 4 * CHUNK + group * LANES + rank - CHUNK
+    edge = lax.broadcasted_iota(I32, (1, slots), 1)
+    one = jnp.ones_like(edge)
+    order = [(n, pair) for n in range(len(lists)) for pair in range(pairs)]
+
+    values, masks = [], []
+    for ref in id_refs:
+        packed = jnp.concatenate([ref[b, round_index : round_index + 1, :] for b in range(blocks)], 0)
+        kinds = jnp.concatenate([ref[b, 2:3, :] for b in range(blocks)], 0)
+        kinds = jnp.bitwise_and(jnp.right_shift(kinds, 16 * round_index), 65535)
+        sides = [jnp.bitwise_and(packed, 65535), jnp.right_shift(packed, 16)]
+        values.append((sides, kinds))
+    spots = []
+    for bucket, side, group in lists:
+        sides, kinds = values[bucket]
+        if round_index == 0:
+            ids = jnp.where(side == 0, sides[0], sides[1])
+        else:
+            ids = sides[side]
+        live = sides[0] != DEAD
+        holder = ids // rows_per
+        local = jnp.where(live, ids - holder * rows_per, 0)
+        if round_index == 0 and len(spots) < 2:
+            mine = holder // 4 * 2 + holder % 2 == group
+            which = holder // 2 % 2
+        else:
+            mine = holder // 2 == group
+            which = holder % 2
+        mine = jnp.logical_and(mine, live)
+        spots.append((local, jnp.where(live, which, 0), mine, kinds))
+        for k in range(2):
+            masks.append(jnp.logical_and(mine, which == k).astype(F32))
+    stacked = jnp.concatenate(masks, 0).astype(BF16)
+    running = jnp.dot(stacked, before, preferred_element_type=F32)
+    slots_of, late = [], []
+    for n, (local, which, mine, kinds) in enumerate(spots):
+        even, odd = (
+            running[(2 * n + k) * blocks : (2 * n + k + 1) * blocks] for k in range(2)
+        )
+        second = lax.broadcasted_iota(I32, (blocks, 1), 0) % 2 == 1
+        totals = [part[:, slots - 1 : slots] for part in (even, odd)]
+        ahead = [
+            jnp.concatenate([total[:1], total[:-1]], 0) for total in totals
+        ]
+        behind = [jnp.concatenate([total[1:], total[:1]], 0) for total in totals]
+        whole = [
+            total + jnp.where(second, a, b) for total, a, b in zip(totals, ahead, behind)
+        ]
+        even = even + jnp.where(second, ahead[0], 0.0)
+        odd = odd + jnp.where(second, ahead[1], 0.0)
+        room = CHUNK - whole[1]
+        slot = jnp.where(
+            which == 1, CHUNK - odd, jnp.where(even <= room, even - 1, CHUNK + even - 1 - room)
+        )
+        slots_of.append(jnp.where(mine, slot, -1.0))
+        bit = lax.broadcasted_iota(I32, (blocks, 1), 0) // 2 + pairs * n
+        over = jnp.logical_and(jnp.logical_not(second), whole[0] > room)
+        late.append(jnp.where(over, jnp.left_shift(jnp.ones_like(bit), bit), 0))
+    late = jnp.sum(jnp.concatenate(late, 0))
+    chunk_ids = lax.broadcasted_iota(I32, (CHUNK, 2 * slots), 0).astype(F32)
+    late_ids = lax.broadcasted_iota(I32, (LANES, 2 * slots), 0).astype(F32) + CHUNK
+    edges = jnp.concatenate([edge, edge + slots], 1)
+    nobody = jnp.full((1, LANES), NOBODY, I32)
+    blank = jnp.zeros((1, LANES), I32)
+    for n, (local, which, mine, kinds) in enumerate(spots):
+        for pair in range(pairs):
+
+            def joined(part, pair=pair):
+                return jnp.concatenate([part[2 * pair : 2 * pair + 1], part[2 * pair + 1 : 2 * pair + 2]], 1)
+
+            slot = joined(slots_of[n])
+            columns = (
+                jnp.concatenate(
+                    [
+                        joined(local),
+                        joined(which),
+                        joined(kinds),
+                        edges // 32,
+                        edges % 32,
+                        jnp.ones_like(edges),
+                    ]
+                    + [jnp.zeros_like(edges)] * 2,
+                    0,
+                )
+                .astype(F32)
+                .astype(BF16)
             )
-            slot = jnp.where(live, slot, -1)
-            joined.append((slot, local, which))
-        slot, local, which = (
-            jnp.concatenate([a, b], 1) for a, b in zip(joined[0], joined[1])
-        )
-        kind = jnp.concatenate(
-            [ref[3 * round_index + 2 : 3 * round_index + 3, :] for ref in (own_ref, other_ref)], 1
-        )
-        values = jnp.concatenate(
-            [local, which, kind, edge // 32, edge % 32, jnp.ones_like(edge)]
-            + [jnp.zeros_like(edge)] * 2,
-            0,
-        ).astype(F32).astype(BF16)
-
-        def place_rows(slot_ids, first_row):
-            pick = (slot_ids == slot).astype(F32).astype(BF16)
-            rows = lax.dot_general(
-                values, pick, (((1,), (1,)), ((), ())), preferred_element_type=F32
-            ).astype(I32)
-            there = rows[5:6] > 0
-            ids = jnp.where(there, rows[1:2] * rows_per + rows[0:1], NOBODY)
-            packed = jnp.bitwise_or(ids, jnp.left_shift(rows[3:4] * 32 + rows[4:5], 16))
-            for at in range(slot_ids.shape[0] // LANES):
-                cut = slice(at * LANES, (at + 1) * LANES)
-                row = first_row + at
-                out_ref[round_index, 2 * side, row : row + 1, :] = packed[:, cut]
-                if side == 0:
-                    out_ref[round_index, 1, row : row + 1, :] = rows[2:3, cut]
-
-        place_rows(main_ids, 0)
-        out_ref[round_index, 2 * side, 8:12, :] = jnp.full((4, LANES), NOBODY, I32)
-        if side == 0:
-            out_ref[round_index, 1, 8:12, :] = jnp.zeros((4, LANES), I32)
-
-        @pl.when(jnp.max(slot) >= 4 * CHUNK)
-        def _():
-            place_rows(rest_ids, 8)
-
-
-def make_lists(own, other, relations, rows_per):
+
+            def rows_at(slot_ids, slot=slot, columns=columns):
+                chosen = (slot_ids == slot).astype(F32).astype(BF16)
+                got = lax.dot_general(
+                    columns, chosen, (((1,), (1,)), ((), ())), preferred_element_type=F32
+                ).astype(I32)
+                ids = jnp.where(got[5:6] > 0, got[1:2] * rows_per + got[0:1], NOBODY)
+                return jnp.bitwise_or(ids, jnp.left_shift(got[3:4] * 32 + got[4:5], 16)), got[2:3]
+
+            packed, kind = rows_at(chunk_ids)
+            for k in range(2):
+                cut = slice(k * LANES, (k + 1) * LANES)
+                out_ref[n, pair, k : k + 1, :] = packed[:, cut]
+                out_ref[n, pair, 3 + k : 4 + k, :] = kind[:, cut]
+            out_ref[n, pair, 2:3, :] = nobody
+            out_ref[n, pair, 5:6, :] = blank
+
+            @pl.when(jnp.bitwise_and(jnp.right_shift(late, pairs * n + pair), 1) > 0)
+            def _():
+                packed, kind = rows_at(late_ids)
+                out_ref[n, pair, 2:3, :] = packed
+                out_ref[n, pair, 5:6, :] = kind
+
+
+def make_lists(round_index, ids, relations, rows_per):
     width = relations.shape[1]
 
     def kernel(*refs):
-        lists_kernel(rows_per, *refs)
-
+        lists_kernel(round_index, rows_per, *refs)
+
+    shapes = [jax.ShapeDtypeStruct((3 + round_index, ids[0].shape[0] // 2, 8, LANES), I32)]
+    if round_index == 0:
+        shapes.append(jax.ShapeDtypeStruct((2 * halves(width)[1], relations.shape[0]), BF16))
     return pl.pallas_call(
         kernel,
-        out_shape=(
-            jax.ShapeDtypeStruct((ROUNDS, 3, 12, LANES), I32),
-            jax.ShapeDtypeStruct((2 * halves(width)[1], relations.shape[0]), BF16),
+        out_shape=tuple(shapes),
+        in_specs=[VMEM] * (len(ids) + 1),
+        out_specs=(VMEM,) * len(shapes),
+        compiler_params=PARAMS,
+        cost_estimate=pl.CostEstimate(
+            flops=4_000_000_000, bytes_accessed=1_000_000, transcendentals=0
         ),
-        in_specs=[VMEM] * 3,
-        out_specs=(VMEM, VMEM),
-        compiler_params=PARAMS,
         name="make_lists",
-    )(own, other, relations)
+    )(*ids, relations)
 
 
 def both(left, right):
@@ -265,35 +320,15 @@
     return source_grad, target_grad
 
 
-def wanted_lists(round_index):
-    x, core, z, y = here()
-    if round_index == 0:
-        line = z // 2 * 2 + y
-        other_line = (1 - z // 2) * 2 + y
-        return [(0, core, line), (0, core, other_line), (0, 1 - core, z)]
-    swap = (z % 2 + z // 2 + y) % 2
-    far = jnp.bitwise_xor(z, jnp.where(x == 0, 3 * swap, 1 + swap))
-    return [(0, 0, z), (0, 1, far), (1, 0, far), (1, 1, z)]
-
-
 def tiles_kernel(round_index, *refs):
-    count = 4 if round_index == 0 else 2
-    list_refs, relations_ref, refs = refs[:count], refs[count], refs[count + 1 :]
+    lists, relations_ref, refs = refs[0], refs[1], refs[2:]
     count = 8 if round_index == 0 else 4
     table_refs, out_refs = refs[:count], refs[count : 2 * count]
-    lists, flags, tables, picks, values, sums = refs[2 * count :]
+    tables, picks, values, sums = refs[2 * count :]
     padded, rows = table_refs[0].shape
-    pairs = lists.shape[1]
+    total, pairs = lists.shape[:2]
     x, core, z, y = here()
     low = z % 2
-    wanted = wanted_lists(round_index)
-    total = len(wanted)
-    for pair in range(pairs):
-        if round_index == 0:
-            lists[0, pair] = list_refs[pair][0]
-        else:
-            lists[0, pair] = list_refs[0][pair]
-            lists[1, pair] = list_refs[1][pair]
 
     def choose(flag, first, second):
         return jnp.where(flag == 0, first, second)
@@ -321,52 +356,84 @@
             lay(n, y, table_refs[first], table_refs[first + 1])
 
     def packed_of(n, pair):
-        bucket, side, group = wanted[n]
-        return jnp.concatenate(
-            [lists[bucket, pair, 2 * side, pl.ds(2 * group + j, 1), :] for j in range(2)], 1
-        )
+        return jnp.concatenate([lists[n, pair, k : k + 1, :] for k in range(2)], 1)
 
     def kinds_of(n, pair):
-        bucket, _, group = wanted[n]
-        return jnp.concatenate(
-            [lists[bucket, pair, 1, pl.ds(2 * group + j, 1), :] for j in range(2)], 1
-        )
-
-    row_ids = lax.broadcasted_iota(I32, (2 * rows, CHUNK), 0)
-
-    def pick_of(packed):
-        return (row_ids == jnp.bitwise_and(packed, 65535)).astype(F32).astype(BF16)
+        return jnp.concatenate([lists[n, pair, 3 + k : 4 + k, :] for k in range(2)], 1)
+
+    def one_hot(size, ids):
+        row_ids = lax.broadcasted_iota(jnp.int16, (size, ids.shape[1]), 0)
+        ids = jnp.where(jnp.logical_and(ids >= 0, ids < size), ids, -1).astype(jnp.int16)
+        return jnp.where(row_ids == ids, jnp.ones((), BF16), jnp.zeros((), BF16))
 
     def relate_of(kinds):
-        slots = lax.broadcasted_iota(I32, (relations_ref.shape[1], kinds.shape[1]), 0)
-        chosen = (slots == kinds).astype(F32).astype(BF16)
+        chosen = one_hot(relations_ref.shape[1], kinds)
         return jnp.dot(relations_ref[...], chosen, preferred_element_type=F32)
 
+    span = pairs * LANES
+
+    def side_ids(n, k):
+        packed = [lists[n, pair, k : k + 1, :] for pair in range(pairs)]
+        return jnp.bitwise_and(jnp.concatenate(packed, 1), 65535)
+
+    lane = lax.broadcasted_iota(I32, (1, LANES), 1)
+    notes = jnp.zeros((1, LANES), I32)
     for n in range(total):
         for pair in range(pairs):
-            cut = slice(pair * CHUNK, (pair + 1) * CHUNK)
-            picks[n, :, cut] = pick_of(packed_of(n, pair))
-        values[n] = jnp.dot(tables[n], picks[n], preferred_element_type=F32).astype(BF16)
+            left, right, late = (
+                jnp.bitwise_and(lists[n, pair, row : row + 1, :], 65535) for row in range(3)
+            )
+            over = jnp.logical_and(left >= rows, left < NOBODY)
+            for bit, lane_at, there in (
+                (2 * n, LANES - 1, over),
+                (2 * n + 1, 0, right < rows),
+                (8 + 4 * n + pair, 0, late < NOBODY),
+            ):
+                there = jnp.logical_and(there, lane == lane_at)
+                notes = jnp.bitwise_or(notes, jnp.where(there, 1 << bit, 0))
+    notes = jnp.sum(notes)
+    crossed = [
+        [jnp.bitwise_and(notes, 1 << (2 * n + k)) != 0 for k in range(2)] for n in range(total)
+    ]
+    for n in range(total):
+        for k in range(2):
+            pick = one_hot(rows, side_ids(n, k) - k * rows)
+            picks[n, k] = pick
+            values[n, :, k * span : (k + 1) * span] = jnp.dot(
+                tables[n, :, k * rows : (k + 1) * rows], pick, preferred_element_type=F32
+            ).astype(BF16)
+    for n in range(total):
+        for k in range(2):
+
+            @pl.when(crossed[n][k])
+            def _():
+                pick = one_hot(rows, side_ids(n, k) - (1 - k) * rows)
+                values[n, :, k * span : (k + 1) * span] += jnp.dot(
+                    tables[n, :, (1 - k) * rows : (2 - k) * rows], pick, preferred_element_type=F32
+                ).astype(BF16)
 
     def compute(pair, sources, targets):
-        cut = slice(pair * CHUNK, (pair + 1) * CHUNK)
+        cuts = [slice(k * span + pair * LANES, k * span + (pair + 1) * LANES) for k in range(2)]
 
         def joined(chosen, get):
             return jnp.concatenate([get(n) for n in chosen], 1)
 
+        def rows_of(chosen):
+            return jnp.concatenate([values[n, :, cut] for n in chosen for cut in cuts], 1)
+
         def edges(chosen):
             return joined(chosen, lambda n: jnp.right_shift(packed_of(n, pair), 16))
 
         got = tile(
-            joined(sources, lambda n: values[n, :, cut]),
-            joined(targets, lambda n: values[n, :, cut]),
+            rows_of(sources),
+            rows_of(targets),
             relate_of(joined(sources, lambda n: kinds_of(n, pair))),
             edges(sources),
             edges(targets),
         )
         for chosen, grads in zip((sources, targets), got):
-            for at, n in enumerate(chosen):
-                values[n, :, cut] = grads[:, at * CHUNK : (at + 1) * CHUNK]
+            for at, (n, cut) in enumerate((n, cut) for n in chosen for cut in cuts):
+                values[n, :, cut] = grads[:, at * LANES : (at + 1) * LANES]
 
     if round_index == 0:
 
@@ -388,69 +455,79 @@
         return lax.dot_general(grads, pick, (((1,), (1,)), ((), ())), preferred_element_type=F32)
 
     for n in range(total):
-        sums[n] = scatter(values[n], picks[n])
-
-    def late_row(n, pair, kind):
-        bucket, _, group = wanted[n]
-        return lists[bucket, pair, kind, pl.ds(8 + group, 1), :]
-
-    def late_ids(n, pair):
-        return jnp.bitwise_and(late_row(n, pair, 2 * wanted[n][1]), 65535)
-
-    lowest = late_ids(0, 0)
+        for k in range(2):
+            sums[n, :, k * rows : (k + 1) * rows] = scatter(
+                values[n, :, k * span : (k + 1) * span], picks[n, k]
+            )
     for n in range(total):
-        for pair in range(pairs):
-            lowest = jnp.minimum(lowest, late_ids(n, pair))
-
-    @pl.when(jnp.min(lowest) < NOBODY)
+        for k in range(2):
+
+            @pl.when(crossed[n][k])
+            def _():
+                pick = one_hot(rows, side_ids(n, k) - (1 - k) * rows)
+                sums[n, :, (1 - k) * rows : (2 - k) * rows] += scatter(
+                    values[n, :, k * span : (k + 1) * span], pick
+                )
+
+    @pl.when(jnp.right_shift(notes, 8) != 0)
     def _():
-        for n in range(total):
-            for pair in range(pairs):
-                flags[n, pair] = (jnp.min(late_ids(n, pair)) < NOBODY).astype(I32)
         spare = jnp.full((1, LANES), NOBODY, I32)
 
-        def one_of(options, at):
-            value = options[0]
-            for n in range(1, len(options)):
-                value = jnp.where(at == n, options[n], value)
-            return value
-
         def each(step, carry):
-            pair, task, combo = step // 6, step // 3 % 2, step % 3
+            pair, task = step // 2, step % 2
             if round_index == 0:
                 chosen = (jnp.where(core == 0, task, 2), jnp.where(core == 0, 2, task))
             else:
                 chosen = (2 * task, 2 * task + 1)
-            late = (combo != 1, combo != 0)
-            due = [
-                jnp.logical_or(jnp.logical_not(late[side]), flags[chosen[side], pair] > 0)
+            has_late = [
+                jnp.bitwise_and(jnp.right_shift(notes, 8 + 4 * chosen[side] + pair), 1)
                 for side in range(2)
             ]
 
-            @pl.when(jnp.logical_and(due[0], due[1]))
+            def combine(combo, carry):
+                late = (jnp.where(combo != 1, 1, 0), jnp.where(combo != 0, 1, 0))
+
+                @pl.when(jnp.logical_and(has_late[0] >= late[0], has_late[1] >= late[1]))
+                def _():
+                    found = []
+                    for side in range(2):
+
+                        def rows_of(first, side=side):
+                            left, right, extra = (
+                                lists[chosen[side], pair, first + row : first + row + 1, :]
+                                for row in range(3)
+                            )
+                            return jnp.where(
+                                late[side] == 0,
+                                jnp.concatenate([left, right], 1),
+                                jnp.concatenate([extra, spare], 1),
+                            )
+
+                        packed = rows_of(0)
+                        pick = one_hot(2 * rows, jnp.bitwise_and(packed, 65535))
+                        gathered = jnp.dot(
+                            tables[chosen[side]], pick, preferred_element_type=F32
+                        ).astype(BF16)
+                        found.append((gathered, pick, jnp.right_shift(packed, 16), rows_of))
+                    grads = tile(
+                        found[0][0],
+                        found[1][0],
+                        relate_of(found[0][3](3)),
+                        found[0][2],
+                        found[1][2],
+                    )
+                    for side in range(2):
+                        sums[chosen[side]] += scatter(grads[side], found[side][1])
+
+                return carry
+
+            @pl.when(has_late[0] + has_late[1] > 0)
             def _():
-                found = []
-                for side in range(2):
-                    main = one_of([packed_of(n, pair) for n in range(total)], chosen[side])
-                    extra = one_of(
-                        [late_row(n, pair, 2 * wanted[n][1]) for n in range(total)], chosen[side]
-                    )
-                    packed = jnp.where(late[side], jnp.concatenate([extra, spare], 1), main)
-                    pick = pick_of(packed)
-                    gathered = jnp.dot(tables[chosen[side]], pick, preferred_element_type=F32)
-                    found.append((gathered.astype(BF16), pick, jnp.right_shift(packed, 16)))
-                main = one_of([kinds_of(n, pair) for n in range(total)], chosen[0])
-                extra = one_of([late_row(n, pair, 1) for n in range(total)], chosen[0])
-                kinds = jnp.where(late[0], jnp.concatenate([extra, extra], 1), main)
-                grads = tile(
-                    found[0][0], found[1][0], relate_of(kinds), found[0][2], found[1][2]
-                )
-                for side in range(2):
-                    sums[chosen[side]] += scatter(grads[side], found[side][1])
+                lax.fori_loop(0, 3, combine, 0)
 
             return carry
 
-        lax.fori_loop(0, pairs * 6, each, 0)
+        lax.fori_loop(0, pairs * 2, each, 0)
 
     def part(total, which):
         return choose(which, total[:, :rows], total[:, rows:])
@@ -489,23 +566,21 @@
 
 def tiles(round_index, lists, relations, tables):
     padded, rows = tables[0].shape
-    total, pairs = 3 + round_index, 4
+    total, pairs = lists.shape[:2]
 
     def kernel(*refs):
         tiles_kernel(round_index, *refs)
 
     kinds = [F32] * 4 + [BF16] * 4 if round_index == 0 else [F32] + [BF16] * 3
-    operands = (*lists, relations, *tables)
+    operands = (lists, relations, *tables)
     return pl.pallas_call(
         kernel,
         out_shape=tuple(jax.ShapeDtypeStruct((padded, rows), kind) for kind in kinds),
         in_specs=[VMEM] * len(operands),
         out_specs=(VMEM,) * len(kinds),
         scratch_shapes=[
-            pltpu.VMEM((2, pairs, 3, 12, LANES), I32),
-            pltpu.SMEM((4, pairs), I32),
             pltpu.VMEM((total, padded, 2 * rows), BF16),
-            pltpu.VMEM((total, 2 * rows, pairs * CHUNK), BF16),
+            pltpu.VMEM((total, 2, rows, pairs * LANES), BF16),
             pltpu.VMEM((total, padded, pairs * CHUNK), BF16),
             pltpu.VMEM((total, padded, 2 * rows), F32),
         ],
@@ -546,36 +621,33 @@
     )(master, state, own, a, b, c)
 
 
-def tied(value, other):
-    return lax.optimization_barrier((value, other))[0]
-
-
 def tile_body(entity_table, adagrad_state, relations, sources, targets, relation_ids, edge_counts):
     rows = entity_table.shape[1]
     entity = entity_table[0].T
     state = adagrad_state
-    wire, ids = open_tables(entity, edge_counts, sources, targets, relation_ids)
-
-    other_ids = move(ids, SWAP_Y)
-    near = [wire] + [move(wire, pairs) for pairs in FIRST]
-    lists, relate = make_lists(ids, other_ids, relations, rows)
-    lists = [lists] + [move(lists, pairs) for pairs in ALONG_Z]
-    *near, _ = lax.optimization_barrier((*near, lists))
+    row_total = lax.axis_size("row")
+    wire, ids = open_tables(entity, edge_counts, sources, targets, relation_ids, row_total)
+    ids = lax.all_to_all(ids, "row", split_axis=0, concat_axis=0, tiled=True)
+    near = [wire, None] + [move(wire, pairs) for pairs in FIRST[1:]]
+    tied_wire, _ = lax.optimization_barrier((wire, ids))
+    near[1] = move(tied_wire, FIRST[0])
+    near[2], near[3], ids = lax.optimization_barrier((near[2], near[3], ids))
+    lists, relate = make_lists(0, [ids], relations, rows)
+    other_ids = move(ids, SWAP_X)
     far = [move(block, SWAP_CORE) for block in near]
-    second_lists = jnp.stack([part[1] for part in lists])
-    other_lists = move(second_lists, SWAP_X)
-
-    first = lax.optimization_barrier((lists, second_lists))[0]
-    outs = tiles(0, first, relate, near + far)
-    outs, other_lists = lax.optimization_barrier((outs, other_lists))
+
+    outs = tiles(0, lists, relate, near + far)
+    outs, ids, other_ids = lax.optimization_barrier((outs, ids, other_ids))
     cross = [move(block, SWAP_CORE).astype(F32) for block in outs[4:]]
-    parts = [
-        move((outs[1 + k] + cross[1 + k]).astype(BF16), back(FIRST[k])) for k in range(3)
-    ]
-    entity, state, wire = update(entity, state, outs[0] + cross[0], *parts, False)
+    sent = [(outs[1 + k] + cross[1 + k]).astype(BF16) for k in range(3)]
+    parts = [move(sent[k], back(FIRST[k])) for k in range(3)]
+    own, ids, other_ids, _ = lax.optimization_barrier((outs[0] + cross[0], ids, other_ids, sent))
+    (lists,) = make_lists(1, [ids, other_ids], relations, rows)
+    entity, lists = lax.optimization_barrier((entity, lists))
+    entity, state, wire = update(entity, state, own, *parts, False)
 
     near = [wire] + [move(wire, pairs) for pairs in SECOND]
-    own, *parts = tiles(1, [second_lists, other_lists], relate, near)
+    own, *parts = tiles(1, lists, relate, near)
     parts = [move(parts[k], back(SECOND[k])) for k in range(3)]
     entity, state = update(entity, state, own, *parts, True)
     return (entity.T[None], state)

time: 85.8 us -> 89.4 us (1.042)
  Pallas kernels: 22.6 us -> 25.5 us
  local copies, waits for them, and re-layouts: 2.4 us -> 0.02 us
  waiting for transfers between devices: 26.9 us -> 29.1 us
    all_to_all x0 -> x1, starting transfers between devices: none -> 6.35 us  [tile_body(): ids = lax.all_to_all(ids, 'row', split_axis=0, concat_axis=0, tiled=True)]
    ppermute x25 -> x21, starting transfers between devices: 32.3 us -> 26.7 us  [move(): return lax.ppermute(value, ('dom', 'row'), pairs)]
    pallas_call x1 -> x2, Pallas kernels: 2.52 us -> 7.94 us  [make_lists(): pl.pallas_call(kernel, out_shape=tuple(shapes), in_specs=[VMEM] * (len(id...]
    pallas_call x2, Pallas kernels: 17.1 us -> 14.5 us  [tiles(): pl.pallas_call(kernel, out_shape=tuple((jax.ShapeDtypeStruct((padded, row...]
    unnamed x18 -> x8, local copies, waits for them, and re-layouts: 1.67 us -> 0.02 us
    all_to_all x0 -> x1, waiting for transfers between devices: none -> 1.49 us  [tile_body(): ids = lax.all_to_all(ids, 'row', split_axis=0, concat_axis=0, tiled=True)]
    ppermute x25 -> x21, waiting for transfers between devices: 26.9 us -> 27.6 us  [move(): return lax.ppermute(value, ('dom', 'row'), pairs)]
  transfers between devices with their start and end apart: 25 -> 22, of which waited for: 12 -> 11; matrix products, arithmetic and copies ran while one was open for 0% -> 0% of each run, Pallas kernels for 12% -> 16%
where the time goes in v1:
time: 89.4 us; the launch traced here: 88.7 us
  starting transfers between devices  33 us (37%)
  waiting for transfers between devices  29.1 us (33%)
  Pallas kernels  25.5 us (29%)
    ppermute x21, waiting for transfers between devices, move(): return lax.ppermute(value, ('dom', 'row'), pairs)  27.6 us
    ppermute x21, starting transfers between devices, move(): return lax.ppermute(value, ('dom', 'row'), pairs)  26.7 us
    pallas_call x2, Pallas kernels, tiles(): pl.pallas_call(kernel, out_shape=tuple((jax.ShapeDtypeStruct((padded, row...  14.5 us
    pallas_call x2, Pallas kernels, make_lists(): pl.pallas_call(kernel, out_shape=tuple(shapes), in_specs=[VMEM] * (len(id...  7.94 us
    all_to_all x1, starting transfers between devices, tile_body(): ids = lax.all_to_all(ids, 'row', split_axis=0, concat_axis=0, tiled=True)  6.35 us
    pallas_call x1, Pallas kernels, open_tables(): pl.pallas_call(open_kernel, out_shape=(jax.ShapeDtypeStruct((2 * padded,...  1.82 us
  transfers between devices with their start and end apart: 22, of which 11 were waited for; matrix products, arithmetic and copies ran while one was open for 0% of the time, Pallas kernels for 16%

profile of v1, /device:TPU:4, one launch (start us, length us, event | category | flops | bytes accessed | tf_op | source)
XLA Modules:
  0.0 88.7 jit_solution(8383456500313487938)
XLA Ops:
  0.6 1.8 %open_tables.1 = (bf16[416,256]{1,0:T(8,128)(2,1)}, s32[8,4,384]{2,1,0:T(4,128)}) custom-call(f32[400,256]{1,0:T(8,128)} %bitcast.7, s32[1,2]{1,0:T(1,128)} %bitcast.9, s32[2,1,384]{2,1,0:T(1,128)} %source_ref.1, s32[2,1,384]{2,1,0:T(1,128)} %target_ref.1, s32[2,1,384]{2,1,0:T(1,128)} %relation_ref.1), custom_call_target="tpu_custom_call" | custom-call | tf_op jit(solution)/shard_map/open_tables/pallas_call | solution.py:112
  2.5 0.0 copy-start.3
  2.5 6.3 %all-to-all-start = ((s32[8,4,384]{2,1,0:T(4,128)}), s32[8,4,384]{2,1,0:T(4,128)S(1)}, u32[]{:S(2)}, u32[]{:S(2)}) async-start(s32[8,4,384]{2,1,0:T(4,128)} %get-tuple-element.43), calls=%async_computation | async-start | bytes 98304 | tf_op jit(solution)/shard_map/all_to_all | solution.py:630
  8.8 2.4 %collective-permute-start = (bf16[416,256]{1,0:T(8,128)(2,1)}, bf16[416,256]{1,0:T(8,128)(2,1)S(1)}, u32[]{:S(2)}, u32[]{:S(2)}) collective-permute-start(bf16[416,256]{1,0:T(8,128)(2,1)} %get-tuple-element.47.refs_2_), channel_id=1, source_target_pairs={{0,4},{1,5},{2,6},{3,7},{4,0},{5,1},{6,2},{7,3},{8,24},{9,25},{10,... | collective-permute-start | bytes 638984 | tf_op jit(solution)/shard_map/ppermute | solution.py:57
  11.2 1.5 %collective-permute-start.1 = (bf16[416,256]{1,0:T(8,128)(2,1)}, bf16[416,256]{1,0:T(8,128)(2,1)S(1)}, u32[]{:S(2)}, u32[]{:S(2)}) collective-permute-start(bf16[416,256]{1,0:T(8,128)(2,1)} %get-tuple-element.47.refs_2_), channel_id=1, source_target_pairs={{0,6},{1,7},{2,4},{3,5},{4,2},{5,3},{6,0},{7,1},{8,25},{9,24},{10,... | collective-permute-start | bytes 638984 | tf_op jit(solution)/shard_map/ppermute | solution.py:57
  12.6 1.5 %all-to-all-done.refs_0_ = s32[8,4,384]{2,1,0:T(4,128)S(1)} async-done(((s32[8,4,384]{2,1,0:T(4,128)}), s32[8,4,384]{2,1,0:T(4,128)S(1)}, u32[]{:S(2)}, u32[]{:S(2)}) %all-to-all-start) | async-done | bytes 49184 | tf_op jit(solution)/shard_map/all_to_all | solution.py:630
  14.1 0.7 collective-permute-start.2
  14.8 0.0 collective-permute-start.3
  14.8 5.9 %collective-permute-done.refs_4_ = bf16[416,256]{1,0:T(8,128)(2,1)S(1)} collective-permute-done((bf16[416,256]{1,0:T(8,128)(2,1)}, bf16[416,256]{1,0:T(8,128)(2,1)S(1)}, u32[]{:S(2)}, u32[]{:S(2)}) %collective-permute-start) | collective-permute-done | bytes 213024 | tf_op jit(solution)/shard_map/ppermute | solution.py:57
  20.7 0.0 collective-permute-done.1.refs_5_
  20.7 0.0 collective-permute-start.5
  20.7 0.5 collective-permute-start.6
  21.2 1.5 %collective-permute-start.7 = (s32[8,4,384]{2,1,0:T(4,128)S(1)}, s32[8,4,384]{2,1,0:T(4,128)S(1)}, u32[]{:S(2)}, u32[]{:S(2)}) collective-permute-start(s32[8,4,384]{2,1,0:T(4,128)S(1)} %all-to-all-done.refs_0_), channel_id=1, source_target_pairs={{0,16},{1,17},{2,18},{3,19},{4,20},{5,21},{6,22},{7,23},{8,24},{9,... | collective-permute-start | bytes 147464 | tf_op jit(solution)/shard_map/ppermute | solution.py:57
  22.7 0.2 collective-permute-done.2.refs_3_
  22.9 0.0 collective-permute-start.4
  22.9 3.4 %make_lists.2 = (s32[3,4,8,128]{3,2,1,0:T(8,128)S(1)}, bf16[416,16]{1,0:T(8,128)(2,1)S(1)}) custom-call(s32[8,4,384]{2,1,0:T(4,128)S(1)} %all-to-all-done.refs_0_, bf16[16,400]{1,0:T(8,128)(2,1)S(1)} %copy-done.3), custom_call_target="tpu_custom_call" | custom-call | flops 4000000000 | bytes 1000000 | tf_op jit(solution)/shard_map/make_lists/pallas_call | solution.py:275
  26.3 0.0 collective-permute-done.3.refs_6_
  26.4 6.3 %tiles.2 = (f32[416,256]{1,0:T(8,128)S(1)}, f32[416,256]{1,0:T(8,128)S(1)}, f32[416,256]{1,0:T(8,128)S(1)}, f32[416,256]{1,0:T(8,128)S(1)}, bf16[416,256]{1,0:T(...) custom-call(s32[3,4,8,128]{3,2,1,0:T(8,128)S(1)} %get-tuple-element.45.ref, ...), custom_call_target="tpu_custom_call" | custom-call | flops 8000000000 | bytes 8000000 | tf_op jit(solution)/shard_map/tiles/pallas_call | solution.py:576
  32.7 4.0 %collective-permute-start.11 = (bf16[416,256]{1,0:T(8,128)(2,1)S(1)}, bf16[416,256]{1,0:T(8,128)(2,1)S(1)}, u32[]{:S(2)}, u32[]{:S(2)}) collective-permute-start(bf16[416,256]{1,0:T(8,128)(2,1)S(1)} %get-tuple-element.67), channel_id=1, source_target_pairs={{0,8},{1,9},{2,10},{3,11},{4,12},{5,13},{6,14},{7,15},{8,0},{9,1},... | collective-permute-start | bytes 638984 | tf_op jit(solution)/shard_map/ppermute | solution.py:57
  36.7 0.1 collective-permute-start.10
  36.8 0.4 collective-permute-start.9
  37.2 0.1 collective-permute-start.8
  37.3 0.5 collective-permute-done.11
  37.8 0.1 add_convert_fusion
  37.9 2.9 %collective-permute-start.14 = (bf16[416,256]{1,0:T(8,128)(2,1)S(1)}, bf16[416,256]{1,0:T(8,128)(2,1)S(1)}, u32[]{:S(2)}, u32[]{:S(2)}) collective-permute-start(bf16[416,256]{1,0:T(8,128)(2,1)S(1)} %add_convert_fusion), channel_id=1, source_target_pairs={{6,0},{7,1},{4,2},{5,3},{2,4},{3,5},{0,6},{1,7},{25,8},{24,9},{27,... | collective-permute-start | bytes 638984 | tf_op jit(solution)/shard_map/ppermute | solution.py:57
  40.8 0.1 add_convert_fusion.1
  40.8 5.9 %collective-permute-start.13 = (bf16[416,256]{1,0:T(8,128)(2,1)S(1)}, bf16[416,256]{1,0:T(8,128)(2,1)S(1)}, u32[]{:S(2)}, u32[]{:S(2)}) collective-permute-start(bf16[416,256]{1,0:T(8,128)(2,1)S(1)} %add_convert_fusion.1), channel_id=1, source_target_pairs={{4,0},{5,1},{6,2},{7,3},{0,4},{1,5},{2,6},{3,7},{24,8},{25,9},{26,... | collective-permute-start | bytes 638984 | tf_op jit(solution)/shard_map/ppermute | solution.py:57
  46.7 0.1 add_convert_fusion.2
  46.7 0.1 collective-permute-start.12
  46.9 0.0 copy-start
  46.9 0.0 copy-start.1
  46.9 4.5 %make_lists.3.refs_0_ = s32[4,4,8,128]{3,2,1,0:T(8,128)S(1)} custom-call(s32[8,4,384]{2,1,0:T(4,128)S(1)} %all-to-all-done.refs_0_, s32[8,4,384]{2,1,0:T(4,128)S(1)} %collective-permute-done.7.refs_1_, bf16[16,400]{1,0:T(8,128)(2,1)S(1)} %copy-done.3), custom_call_target="tpu_custom_call" | custom-call | flops 4000000000 | bytes 1000000 | tf_op jit(solution)/shard_map/make_lists/pallas_call | solution.py:275
  51.4 5.7 %collective-permute-done.13.b_ref = bf16[416,256]{1,0:T(8,128)(2,1)S(1)} collective-permute-done((bf16[416,256]{1,0:T(8,128)(2,1)S(1)}, bf16[416,256]{1,0:T(8,128)(2,1)S(1)}, u32[]{:S(2)}, u32[]{:S(2)}) %collective-permute-start.13) | collective-permute-done | bytes 213024 | tf_op jit(solution)/shard_map/ppermute | solution.py:57
  57.2 0.2 update.2
  57.4 0.1 collective-permute-start.15
  57.5 0.1 collective-permute-start.16
  57.5 1.4 %collective-permute-start.17 = (bf16[416,256]{1,0:T(8,128)(2,1)S(1)}, bf16[416,256]{1,0:T(8,128)(2,1)S(1)}, u32[]{:S(2)}, u32[]{:S(2)}) collective-permute-start(bf16[416,256]{1,0:T(8,128)(2,1)S(1)} %get-tuple-element.75.refs_2_), channel_id=1, source_target_pairs={{17,0},{22,1},{21,2},{18,3},{19,4},{20,5},{23,6},{16,7},{25,8},{30... | collective-permute-start | bytes 638984 | tf_op jit(solution)/shard_map/ppermute | solution.py:57
  59.0 5.2 %collective-permute-done.15.refs_3_ = bf16[416,256]{1,0:T(8,128)(2,1)S(1)} collective-permute-done((bf16[416,256]{1,0:T(8,128)(2,1)S(1)}, bf16[416,256]{1,0:T(8,128)(2,1)S(1)}, u32[]{:S(2)}, u32[]{:S(2)}) %collective-permute-start.15) | collective-permute-done | bytes 213024 | tf_op jit(solution)/shard_map/ppermute | solution.py:57
  64.2 1.9 %collective-permute-done.16.refs_4_ = bf16[416,256]{1,0:T(8,128)(2,1)S(1)} collective-permute-done((bf16[416,256]{1,0:T(8,128)(2,1)S(1)}, bf16[416,256]{1,0:T(8,128)(2,1)S(1)}, u32[]{:S(2)}, u32[]{:S(2)}) %collective-permute-start.16) | collective-permute-done | bytes 213024 | tf_op jit(solution)/shard_map/ppermute | solution.py:57
  66.2 1.0 %collective-permute-done.17.refs_5_ = bf16[416,256]{1,0:T(8,128)(2,1)S(1)} collective-permute-done((bf16[416,256]{1,0:T(8,128)(2,1)S(1)}, bf16[416,256]{1,0:T(8,128)(2,1)S(1)}, u32[]{:S(2)}, u32[]{:S(2)}) %collective-permute-start.17) | collective-permute-done | bytes 213024 | tf_op jit(solution)/shard_map/ppermute | solution.py:57
  67.1 8.2 %tiles.3 = (f32[416,256]{1,0:T(8,128)S(1)}, bf16[416,256]{1,0:T(8,128)(2,1)S(1)}, bf16[416,256]{1,0:T(8,128)(2,1)S(1)}, bf16[416,256]{1,0:T(8,128)(2,1)S(1)}) custom-call(s32[4,4,8,128]{3,2,1,0:T(8,128)S(1)} %make_lists.3.refs_0_, bf16[416,16]{1,0:T(8,128)(2,1)S(1)} %get-tuple-element.46.refs_1_, bf16[416,256]{1,0:T(8,128)(2,1)S(1)} %get-tuple-element.75.refs_2_, ...), custom_call_target="tpu_custom_call" | custom-call | flops 8000000000 | bytes 8000000 | tf_op jit(solution)/shard_map/tiles/pallas_call | solution.py:576
  75.4 1.4 %collective-permute-start.18 = (bf16[416,256]{1,0:T(8,128)(2,1)S(1)}, bf16[416,256]{1,0:T(8,128)(2,1)S(1)}, u32[]{:S(2)}, u32[]{:S(2)}) collective-permute-start(bf16[416,256]{1,0:T(8,128)(2,1)S(1)} %get-tuple-element.77), channel_id=1, source_target_pairs={{1,0},{0,1},{3,2},{2,3},{5,4},{4,5},{7,6},{6,7},{9,8},{8,9},{11,10... | collective-permute-start | bytes 638984 | tf_op jit(solution)/shard_map/ppermute | solution.py:57
  76.8 2.4 %collective-permute-start.19 = (bf16[416,256]{1,0:T(8,128)(2,1)S(1)}, bf16[416,256]{1,0:T(8,128)(2,1)S(1)}, u32[]{:S(2)}, u32[]{:S(2)}) collective-permute-start(bf16[416,256]{1,0:T(8,128)(2,1)S(1)} %get-tuple-element.78), channel_id=1, source_target_pairs={{0,16},{1,23},{2,20},{3,19},{4,18},{5,21},{6,22},{7,17},{8,24},{9,... | collective-permute-start | bytes 638984 | tf_op jit(solution)/shard_map/ppermute | solution.py:57
  79.2 1.4 %collective-permute-start.20 = (bf16[416,256]{1,0:T(8,128)(2,1)S(1)}, bf16[416,256]{1,0:T(8,128)(2,1)S(1)}, u32[]{:S(2)}, u32[]{:S(2)}) collective-permute-start(bf16[416,256]{1,0:T(8,128)(2,1)S(1)} %get-tuple-element.79), channel_id=1, source_target_pairs={{0,17},{1,22},{2,21},{3,18},{4,19},{5,20},{6,23},{7,16},{8,25},{9,... | collective-permute-start | bytes 638984 | tf_op jit(solution)/shard_map/ppermute | solution.py:57
  80.6 2.6 %collective-permute-done.18.a_ref = bf16[416,256]{1,0:T(8,128)(2,1)S(1)} collective-permute-done((bf16[416,256]{1,0:T(8,128)(2,1)S(1)}, bf16[416,256]{1,0:T(8,128)(2,1)S(1)}, u32[]{:S(2)}, u32[]{:S(2)}) %collective-permute-start.18) | collective-permute-done | bytes 213024 | tf_op jit(solution)/shard_map/ppermute | solution.py:57
  83.2 0.4 collective-permute-done.19.b_ref
  83.6 4.2 %collective-permute-done.20.c_ref = bf16[416,256]{1,0:T(8,128)(2,1)S(1)} collective-permute-done((bf16[416,256]{1,0:T(8,128)(2,1)S(1)}, bf16[416,256]{1,0:T(8,128)(2,1)S(1)}, u32[]{:S(2)}, u32[]{:S(2)}) %collective-permute-start.20) | collective-permute-done | bytes 213024 | tf_op jit(solution)/shard_map/ppermute | solution.py:57
  87.7 1.0 %update.3 = (f32[400,256]{1,0:T(8,128)}, f32[1,256]{1,0:T(1,128)}) custom-call(f32[400,256]{1,0:T(8,128)S(1)} %get-tuple-element.72.master_ref, f32[1,256]{1,0:T(1,128)S(1)} %get-tuple-element.73.state_ref, f32[416,256]{1,0:T(8,128)S(1)} %get-tuple-element.76.own_ref, bf16[416,256]{1,0:T(8,128)(2,1)S(1)} %collective-permute-done.18.a_ref, ...), custom_call_target="tpu_custom_call" | custom-call | tf_op jit(solution)/shard_map/update/pallas_call | solution.py:614
  (15 shorter events, 0.1 us)
Async XLA Ops:
  2.5 20.4 %copy-start.3 = (bf16[16,400]{1,0:T(8,128)(2,1)S(1)}, bf16[16,400]{1,0:T(8,128)(2,1)}, u32[]{:S(2)}) copy-start(bf16[16,400]{1,0:T(8,128)(2,1)} %refs_2_.1) | copy-start | bytes 38404
  2.5 11.7 %all-to-all-start = ((s32[8,4,384]{2,1,0:T(4,128)}), s32[8,4,384]{2,1,0:T(4,128)S(1)}, u32[]{:S(2)}, u32[]{:S(2)}) async-start(s32[8,4,384]{2,1,0:T(4,128)} %get-tuple-element.43), calls=%async_computation | async-start | bytes 98304 | tf_op jit(solution)/shard_map/all_to_all | solution.py:630
  8.8 17.6 %copy-start.2 = (bf16[416,256]{1,0:T(8,128)(2,1)S(1)}, bf16[416,256]{1,0:T(8,128)(2,1)}, u32[]{:S(2)}) copy-start(bf16[416,256]{1,0:T(8,128)(2,1)} %get-tuple-element.47.refs_2_) | copy-start | bytes 638980
  8.8 11.9 %collective-permute-start = (bf16[416,256]{1,0:T(8,128)(2,1)}, bf16[416,256]{1,0:T(8,128)(2,1)S(1)}, u32[]{:S(2)}, u32[]{:S(2)}) collective-permute-start(bf16[416,256]{1,0:T(8,128)(2,1)} %get-tuple-element.47.refs_2_), channel_id=1, source_target_pairs={{0,4},{1,5},{2,6},{3,7},{4,0},{5,1},{6,2},{7,3},{8,24},{9,25},{10,... | collective-permute-start | bytes 638984 | tf_op jit(solution)/shard_map/ppermute | solution.py:57
  11.2 9.5 %collective-permute-start.1 = (bf16[416,256]{1,0:T(8,128)(2,1)}, bf16[416,256]{1,0:T(8,128)(2,1)S(1)}, u32[]{:S(2)}, u32[]{:S(2)}) collective-permute-start(bf16[416,256]{1,0:T(8,128)(2,1)} %get-tuple-element.47.refs_2_), channel_id=1, source_target_pairs={{0,6},{1,7},{2,4},{3,5},{4,2},{5,3},{6,0},{7,1},{8,25},{9,24},{10,... | collective-permute-start | bytes 638984 | tf_op jit(solution)/shard_map/ppermute | solution.py:57
  14.1 8.7 %collective-permute-start.2 = (bf16[416,256]{1,0:T(8,128)(2,1)}, bf16[416,256]{1,0:T(8,128)(2,1)S(1)}, u32[]{:S(2)}, u32[]{:S(2)}) collective-permute-start(bf16[416,256]{1,0:T(8,128)(2,1)} %get-tuple-element.47.refs_2_), channel_id=1, source_target_pairs={{0,2},{1,3},{2,0},{3,1},{4,6},{5,7},{6,4},{7,5},{8,9},{9,8},{10,11... | collective-permute-start | bytes 638984 | tf_op jit(solution)/shard_map/ppermute | solution.py:57
  14.8 11.5 %collective-permute-start.3 = (bf16[416,256]{1,0:T(8,128)(2,1)}, bf16[416,256]{1,0:T(8,128)(2,1)S(1)}, u32[]{:S(2)}, u32[]{:S(2)}) collective-permute-start(bf16[416,256]{1,0:T(8,128)(2,1)} %get-tuple-element.47.refs_2_), channel_id=1, source_target_pairs={{0,8},{1,9},{2,10},{3,11},{4,12},{5,13},{6,14},{7,15},{8,0},{9,1},... | collective-permute-start | bytes 638984 | tf_op jit(solution)/shard_map/ppermute | solution.py:57
  20.7 5.6 %collective-permute-start.5 = (bf16[416,256]{1,0:T(8,128)(2,1)S(1)}, bf16[416,256]{1,0:T(8,128)(2,1)S(1)}, u32[]{:S(2)}, u32[]{:S(2)}) collective-permute-start(bf16[416,256]{1,0:T(8,128)(2,1)S(1)} %collective-permute-done.refs_4_), channel_id=1, source_target_pairs={{0,8},{1,9},{2,10},{3,11},{4,12},{5,13},{6,14},{7,15},{8,0},{9,1},... | collective-permute-start | bytes 638984 | tf_op jit(solution)/shard_map/ppermute | solution.py:57
  20.7 5.6 %collective-permute-start.6 = (bf16[416,256]{1,0:T(8,128)(2,1)S(1)}, bf16[416,256]{1,0:T(8,128)(2,1)S(1)}, u32[]{:S(2)}, u32[]{:S(2)}) collective-permute-start(bf16[416,256]{1,0:T(8,128)(2,1)S(1)} %collective-permute-done.1.refs_5_), channel_id=1, source_target_pairs={{0,8},{1,9},{2,10},{3,11},{4,12},{5,13},{6,14},{7,15},{8,0},{9,1},... | collective-permute-start | bytes 638984 | tf_op jit(solution)/shard_map/ppermute | solution.py:57
  21.2 11.5 %collective-permute-start.7 = (s32[8,4,384]{2,1,0:T(4,128)S(1)}, s32[8,4,384]{2,1,0:T(4,128)S(1)}, u32[]{:S(2)}, u32[]{:S(2)}) collective-permute-start(s32[8,4,384]{2,1,0:T(4,128)S(1)} %all-to-all-done.refs_0_), channel_id=1, source_target_pairs={{0,16},{1,17},{2,18},{3,19},{4,20},{5,21},{6,22},{7,23},{8,24},{9,... | collective-permute-start | bytes 147464 | tf_op jit(solution)/shard_map/ppermute | solution.py:57
  22.9 3.5 %collective-permute-start.4 = (bf16[416,256]{1,0:T(8,128)(2,1)S(1)}, bf16[416,256]{1,0:T(8,128)(2,1)S(1)}, u32[]{:S(2)}, u32[]{:S(2)}) collective-permute-start(bf16[416,256]{1,0:T(8,128)(2,1)S(1)} %collective-permute-done.2.refs_3_), channel_id=1, source_target_pairs={{0,8},{1,9},{2,10},{3,11},{4,12},{5,13},{6,14},{7,15},{8,0},{9,1},... | collective-permute-start | bytes 638984 | tf_op jit(solution)/shard_map/ppermute | solution.py:57
  32.7 5.1 %collective-permute-start.11 = (bf16[416,256]{1,0:T(8,128)(2,1)S(1)}, bf16[416,256]{1,0:T(8,128)(2,1)S(1)}, u32[]{:S(2)}, u32[]{:S(2)}) collective-permute-start(bf16[416,256]{1,0:T(8,128)(2,1)S(1)} %get-tuple-element.67), channel_id=1, source_target_pairs={{0,8},{1,9},{2,10},{3,11},{4,12},{5,13},{6,14},{7,15},{8,0},{9,1},... | collective-permute-start | bytes 638984 | tf_op jit(solution)/shard_map/ppermute | solution.py:57
  36.7 4.0 %collective-permute-start.10 = (bf16[416,256]{1,0:T(8,128)(2,1)S(1)}, bf16[416,256]{1,0:T(8,128)(2,1)S(1)}, u32[]{:S(2)}, u32[]{:S(2)}) collective-permute-start(bf16[416,256]{1,0:T(8,128)(2,1)S(1)} %get-tuple-element.65), channel_id=1, source_target_pairs={{0,8},{1,9},{2,10},{3,11},{4,12},{5,13},{6,14},{7,15},{8,0},{9,1},... | collective-permute-start | bytes 638984 | tf_op jit(solution)/shard_map/ppermute | solution.py:57
  36.8 9.9 %collective-permute-start.9 = (bf16[416,256]{1,0:T(8,128)(2,1)S(1)}, bf16[416,256]{1,0:T(8,128)(2,1)S(1)}, u32[]{:S(2)}, u32[]{:S(2)}) collective-permute-start(bf16[416,256]{1,0:T(8,128)(2,1)S(1)} %get-tuple-element.63), channel_id=1, source_target_pairs={{0,8},{1,9},{2,10},{3,11},{4,12},{5,13},{6,14},{7,15},{8,0},{9,1},... | collective-permute-start | bytes 638984 | tf_op jit(solution)/shard_map/ppermute | solution.py:57
  37.2 9.6 %collective-permute-start.8 = (bf16[416,256]{1,0:T(8,128)(2,1)S(1)}, bf16[416,256]{1,0:T(8,128)(2,1)S(1)}, u32[]{:S(2)}, u32[]{:S(2)}) collective-permute-start(bf16[416,256]{1,0:T(8,128)(2,1)S(1)} %get-tuple-element.59), channel_id=1, source_target_pairs={{0,8},{1,9},{2,10},{3,11},{4,12},{5,13},{6,14},{7,15},{8,0},{9,1},... | collective-permute-start | bytes 638984 | tf_op jit(solution)/shard_map/ppermute | solution.py:57
  37.9 13.6 %collective-permute-start.14 = (bf16[416,256]{1,0:T(8,128)(2,1)S(1)}, bf16[416,256]{1,0:T(8,128)(2,1)S(1)}, u32[]{:S(2)}, u32[]{:S(2)}) collective-permute-start(bf16[416,256]{1,0:T(8,128)(2,1)S(1)} %add_convert_fusion), channel_id=1, source_target_pairs={{6,0},{7,1},{4,2},{5,3},{2,4},{3,5},{0,6},{1,7},{25,8},{24,9},{27,... | collective-permute-start | bytes 638984 | tf_op jit(solution)/shard_map/ppermute | solution.py:57
  40.8 16.3 %collective-permute-start.13 = (bf16[416,256]{1,0:T(8,128)(2,1)S(1)}, bf16[416,256]{1,0:T(8,128)(2,1)S(1)}, u32[]{:S(2)}, u32[]{:S(2)}) collective-permute-start(bf16[416,256]{1,0:T(8,128)(2,1)S(1)} %add_convert_fusion.1), channel_id=1, source_target_pairs={{4,0},{5,1},{6,2},{7,3},{0,4},{1,5},{2,6},{3,7},{24,8},{25,9},{26,... | collective-permute-start | bytes 638984 | tf_op jit(solution)/shard_map/ppermute | solution.py:57
  46.7 10.4 %collective-permute-start.12 = (bf16[416,256]{1,0:T(8,128)(2,1)S(1)}, bf16[416,256]{1,0:T(8,128)(2,1)S(1)}, u32[]{:S(2)}, u32[]{:S(2)}) collective-permute-start(bf16[416,256]{1,0:T(8,128)(2,1)S(1)} %add_convert_fusion.2), channel_id=1, source_target_pairs={{2,0},{3,1},{0,2},{1,3},{6,4},{7,5},{4,6},{5,7},{9,8},{8,9},{11,10... | collective-permute-start | bytes 638984 | tf_op jit(solution)/shard_map/ppermute | solution.py:57
  46.9 10.3 %copy-start = (f32[1,256,400]{1,2,0:T(8,128)S(1)}, f32[1,256,400]{1,2,0:T(8,128)}, u32[]{:S(2)}) copy-start(f32[1,256,400]{1,2,0:T(8,128)} %param.7) | copy-start | bytes 1228804
  46.9 10.3 %copy-start.1 = (f32[1,256]{1,0:T(1,128)S(1)}, f32[1,256]{1,0:T(1,128)}, u32[]{:S(2)}) copy-start(f32[1,256]{1,0:T(1,128)} %state_ref.1) | copy-start | bytes 3076
  57.4 6.8 %collective-permute-start.15 = (bf16[416,256]{1,0:T(8,128)(2,1)S(1)}, bf16[416,256]{1,0:T(8,128)(2,1)S(1)}, u32[]{:S(2)}, u32[]{:S(2)}) collective-permute-start(bf16[416,256]{1,0:T(8,128)(2,1)S(1)} %get-tuple-element.75.refs_2_), channel_id=1, source_target_pairs={{0,1},{1,0},{2,3},{3,2},{4,5},{5,4},{6,7},{7,6},{8,9},{9,8},{10,11... | collective-permute-start | bytes 638984 | tf_op jit(solution)/shard_map/ppermute | solution.py:57
  57.5 8.7 %collective-permute-start.16 = (bf16[416,256]{1,0:T(8,128)(2,1)S(1)}, bf16[416,256]{1,0:T(8,128)(2,1)S(1)}, u32[]{:S(2)}, u32[]{:S(2)}) collective-permute-start(bf16[416,256]{1,0:T(8,128)(2,1)S(1)} %get-tuple-element.75.refs_2_), channel_id=1, source_target_pairs={{16,0},{23,1},{20,2},{19,3},{18,4},{21,5},{22,6},{17,7},{24,8},{31... | collective-permute-start | bytes 638984 | tf_op jit(solution)/shard_map/ppermute | solution.py:57
  57.5 9.6 %collective-permute-start.17 = (bf16[416,256]{1,0:T(8,128)(2,1)S(1)}, bf16[416,256]{1,0:T(8,128)(2,1)S(1)}, u32[]{:S(2)}, u32[]{:S(2)}) collective-permute-start(bf16[416,256]{1,0:T(8,128)(2,1)S(1)} %get-tuple-element.75.refs_2_), channel_id=1, source_target_pairs={{17,0},{22,1},{21,2},{18,3},{19,4},{20,5},{23,6},{16,7},{25,8},{30... | collective-permute-start | bytes 638984 | tf_op jit(solution)/shard_map/ppermute | solution.py:57
  75.4 7.8 %collective-permute-start.18 = (bf16[416,256]{1,0:T(8,128)(2,1)S(1)}, bf16[416,256]{1,0:T(8,128)(2,1)S(1)}, u32[]{:S(2)}, u32[]{:S(2)}) collective-permute-start(bf16[416,256]{1,0:T(8,128)(2,1)S(1)} %get-tuple-element.77), channel_id=1, source_target_pairs={{1,0},{0,1},{3,2},{2,3},{5,4},{4,5},{7,6},{6,7},{9,8},{8,9},{11,10... | collective-permute-start | bytes 638984 | tf_op jit(solution)/shard_map/ppermute | solution.py:57
  76.8 6.7 %collective-permute-start.19 = (bf16[416,256]{1,0:T(8,128)(2,1)S(1)}, bf16[416,256]{1,0:T(8,128)(2,1)S(1)}, u32[]{:S(2)}, u32[]{:S(2)}) collective-permute-start(bf16[416,256]{1,0:T(8,128)(2,1)S(1)} %get-tuple-element.78), channel_id=1, source_target_pairs={{0,16},{1,23},{2,20},{3,19},{4,18},{5,21},{6,22},{7,17},{8,24},{9,... | collective-permute-start | bytes 638984 | tf_op jit(solution)/shard_map/ppermute | solution.py:57
  79.2 8.6 %collective-permute-start.20 = (bf16[416,256]{1,0:T(8,128)(2,1)S(1)}, bf16[416,256]{1,0:T(8,128)(2,1)S(1)}, u32[]{:S(2)}, u32[]{:S(2)}) collective-permute-start(bf16[416,256]{1,0:T(8,128)(2,1)S(1)} %get-tuple-element.79), channel_id=1, source_target_pairs={{0,17},{1,22},{2,21},{3,18},{4,19},{5,20},{6,23},{7,16},{8,25},{9,... | collective-permute-start | bytes 638984 | tf_op jit(solution)/shard_map/ppermute | solution.py:57
